TPU v7x, 32 devices: a whole 2x2x4 slice. The times are simulated.
32 devices in a mesh: grp: 4 (over z), blk: 8 (over y, x, core).
Axes of the slice: x: 2, y: 2, z: 4, core: 2. Of those that a mesh axis runs over, the one named last changes fastest.
Arguments:
- ancestor_inv: float32 [4, 6144, 3072], P('grp', 'blk'), as said below
- lower_block: float32 [4, 3840, 768], P('grp', 'blk'), may hold values from -0.009765625 to 0.009765625
- diag_inverse: float32 [4, 768, 768], P('grp', 'blk'), as said below
- row_index: int32 [4, 3840], P('grp'), may hold values from 0 to 6143, as said below
Outputs:
- sigma_rows: float32 [4, 3840, 768], P('grp', 'blk')
- sigma_diag: float32 [4, 768, 768], P('grp', 'blk')
Inputs may be any that keep to these rules, and one draw needn't show every extreme that they name: `row_index`: for each child front: sorted increasing and distinct; exactly 480 entries fall in each aligned block of 768 consecutive indices, among them the block's first and last index. `diag_inverse`: lower triangular with a positive diagonal. `ancestor_inv`: each parent matrix assembled from its two column halves is symmetric.
All inputs are finite; a program needn't handle non-finite values.
Results may differ from a plain program's by a relative error of at most 0.0003.
Values sent between devices are 32-bit elements; how exact they have to be, the bound alone decides.
No kernel may reach another device: no remote copies, remote signals or barrier semaphores. Data moves between devices by JAX's collectives and lax.ppermute only.
A program may use at most 128 MiB of HBM per device.

v0:
```python
import jax
import jax.numpy as jnp
from jax import lax
from jax.sharding import PartitionSpec as P


def partner(x, axis, stride):
    return lax.ppermute(x, axis, [(i, i ^ 1 << stride) for i in range(lax.axis_size(axis))])


def shards(ancestor_inv, lower_block, diag_inverse, row_index):
    highest = lax.Precision.HIGHEST
    blk_count = lax.axis_size("blk")
    tile_rows = ancestor_inv.shape[1]
    half_cols = ancestor_inv.shape[2]
    tile = ancestor_inv[0]
    listed = row_index[0]
    total_rows = listed.shape[0]
    picked = total_rows // blk_count
    half_rows = total_rows // 2
    blk_here = lax.axis_index("blk")
    side = lax.axis_index("grp") % 2
    other_side = 1 - side

    def pick_panel(source, names, col_side):
        rows_here = (
            lax.dynamic_slice_in_dim(names, blk_here * picked, picked) - blk_here * tile_rows
        )
        cols_here = (
            lax.dynamic_slice_in_dim(names, col_side * half_rows, half_rows) - col_side * half_cols
        )
        return jnp.take(jnp.take(source, rows_here, axis=0), cols_here, axis=1)

    own_part = pick_panel(tile, listed, side)
    partner_tile = partner(tile, "grp", 0)
    other_part = pick_panel(partner_tile, listed, other_side)
    low_first = jnp.concatenate([own_part, other_part], axis=1)
    high_first = jnp.concatenate([other_part, own_part], axis=1)
    row_panel = jnp.where(side == 0, low_first, high_first)
    pivot_full = lax.all_gather(diag_inverse, "blk", axis=1, tiled=True)
    factor = jnp.einsum("kra,kab->krb", lower_block, pivot_full, precision=highest)
    product = jnp.einsum(
        "rn,knb->krb",
        row_panel,
        lax.all_gather(factor, "blk", axis=1, tiled=True),
        precision=highest,
    )
    sigma_rows = -product
    cross_terms = jnp.einsum("krb,krc->kbc", factor, sigma_rows, precision=highest)
    reduced = lax.psum_scatter(cross_terms, "blk", scatter_dimension=1, tiled=True)
    row_width = reduced.shape[1]
    gram_cols = lax.dynamic_slice_in_dim(pivot_full, blk_here * row_width, row_width, 2)
    gram_rows = jnp.einsum("kar,kac->krc", gram_cols, pivot_full, precision=highest)
    sigma_diag = gram_rows - reduced
    return (sigma_rows, sigma_diag)


def solution(mesh):
    in_specs = (P("grp", "blk", None), P("grp", "blk", None), P("grp", "blk", None), P("grp", None))
    out_specs = (P("grp", "blk", None), P("grp", "blk", None))
    return jax.shard_map(shards, mesh=mesh, in_specs=in_specs, out_specs=out_specs, check_vma=False)
```

profile of v0, /device:TPU:0, one launch (start us, length us, event | category | flops | bytes accessed | tf_op | source)
XLA Modules:
  0.0 402.6 jit_solution(17657156194829921596)
XLA Ops:
  7.2 0.0 all-gather.4.cloned.1.call-start
  7.2 0.7 all-gather.4.cloned.1.call-update
  7.9 0.0 all-gather.6.cloned.1.call-start
  8.0 33.7 %all-gather.4.cloned.1.call-done = f32[1,768,768]{2,1,0:T(8,128)} async-done(((f32[1,96,768]{2,1,0:T(8,128)}), f32[1,768,768]{2,1,0:T(8,128)}) %all-gather.4.cloned.1.call-update) | async-done | bytes 2359312 | tf_op jit(solution)/shard_map/all_gather | solution.py:40
  41.7 6.5 %fusion.9 = f32[480,768]{1,0:T(8,128)} fusion(f32[1,768,768]{2,1,0:T(8,128)} %all-gather.4.cloned.1.call-done, f32[1,480,768]{2,1,0:T(8,128)S(1)} %copy-done), kind=kOutput, calls=%fused_computation.18 | convolution fusion | flops 3397386240 | bytes 5308416 | tf_op jit(solution)/shard_map/kra,kab->krb/dot_general | solution.py:41
  48.2 0.0 all-gather.6.cloned.1.call-update
  48.2 0.2 reduce-scatter.2.cloned.1.call-start
  48.4 1.6 collective-permute-start
  50.0 0.1 dynamic-slice_subtract_fusion
  50.1 10.9 %gather_fusion = f32[480,3072]{1,0:T(8,128)} fusion(f32[768,3072]{1,0:T(8,128)} %bitcast.37, s32[1024]{0:T(1024)S(1)} %pad_clamp_fusion.2), kind=kCustom, calls=%fused_computation.clone | custom fusion | bytes 11798400 | tf_op jit(solution)/shard_map/jit(_take)/gather | solution.py:32
  61.1 192.8 %collective-permute-done = f32[768,3072]{1,0:T(8,128)} collective-permute-done((f32[768,3072]{1,0:T(8,128)}, f32[768,3072]{1,0:T(8,128)}, u32[]{:S(2)}, u32[]{:S(2)}) %collective-permute-start) | collective-permute-done | bytes 9437216 | tf_op jit(solution)/shard_map/ppermute | solution.py:8
  253.9 10.8 %gather_fusion.2 = f32[480,3072]{1,0:T(8,128)} fusion(f32[768,3072]{1,0:T(8,128)} %collective-permute-done, s32[1024]{0:T(1024)S(1)} %pad_clamp_fusion.2), kind=kCustom, calls=%fused_computation.2.clone | custom fusion | bytes 11798400 | tf_op jit(solution)/shard_map/jit(_take)/gather | solution.py:32
  264.7 11.3 %broadcast_select_fusion.1 = (f32[480,3072]{1,0:T(8,128)}, f32[480,3072]{1,0:T(8,128)}) fusion(f32[480,3072]{1,0:T(8,128)} %gather_fusion, pred[480]{0:T(512)(128)(4,1)S(1)} %compare_and_fusion.2, f32[480,3072]{1,0:T(8,128)} %gather_fusion.2), kind=kLoop, calls=%fused_computation.15 | loop fusion | flops 2949120 | bytes 23593440 | tf_op jit(solution)/shard_map/jit(_take)/select_n | solution.py:32
  276.1 6.5 %copy.6 = f32[480,3072]{0,1:T(8,128)} copy(f32[480,3072]{1,0:T(8,128)} %get-tuple-element.6) | data formatting | bytes 11796480 | tf_op jit(solution)/shard_map/jit(_take)/select_n | solution.py:32
  282.5 6.5 %copy.7 = f32[480,3072]{0,1:T(8,128)} copy(f32[480,3072]{1,0:T(8,128)} %get-tuple-element.7) | data formatting | bytes 11796480 | tf_op jit(solution)/shard_map/jit(_take)/select_n | solution.py:32
  289.1 9.9 %gather_fusion.1 = f32[1920,480]{1,0:T(8,128)} fusion(f32[480,3072]{0,1:T(8,128)} %copy.6, s32[2048]{0:T(1024)S(1)} %pad_clamp_fusion.1), kind=kCustom, calls=%fused_computation.1.clone | custom fusion | bytes 7380480 | tf_op jit(solution)/shard_map/jit(_take)/gather | solution.py:32
  299.0 9.9 %gather_fusion.3 = f32[1920,480]{1,0:T(8,128)} fusion(f32[480,3072]{0,1:T(8,128)} %copy.7, s32[2048]{0:T(1024)S(1)} %pad_clamp_fusion), kind=kCustom, calls=%fused_computation.3.clone | custom fusion | bytes 7380480 | tf_op jit(solution)/shard_map/jit(_take)/gather | solution.py:32
  308.9 4.5 %select_bitcast_fusion.1 = f32[480,1920]{0,1:T(8,128)} fusion(f32[1920,480]{1,0:T(8,128)} %gather_fusion.1, pred[1920]{0:T(1024)(128)(4,1)S(1)} %get-tuple-element.11), kind=kLoop, calls=%fused_computation.12 | loop fusion | flops 921600 | bytes 7374720 | tf_op jit(solution)/shard_map/jit(_take)/select_n | solution.py:32
  313.4 2.3 select_bitcast_fusion
  315.7 26.8 %fusion.13 = f32[768,480]{0,1:T(8,128)S(1)} fusion(f32[3840,768]{1,0:T(8,128)} %all-gather.6.cloned.1.call-done, f32[480,1920]{0,1:T(8,128)} %select_bitcast_fusion, f32[480,1920]{0,1:T(8,128)} %select_bitcast_fusion.1, pred[]{:T(512)S(6)} %eq.5), kind=kOutput, calls=%fused_computation.23 | convolution fusion | flops 16992829440 | bytes 20643840 | tf_op jit(solution)/shard_map/rn,knb->krb/dot_general | solution.py:42
  342.5 1.1 copy-done.4
  343.6 5.6 %convolution_bitcast_fusion = f32[1,768,768]{2,1,0:T(8,128)} fusion(f32[480,768]{1,0:T(8,128)S(1)} %copy-done.3, f32[768,480]{0,1:T(8,128)S(1)} %fusion.13), kind=kOutput, calls=%fused_computation.20 | convolution fusion | flops 3397386240 | bytes 5308416 | tf_op jit(solution)/shard_map/krb,krc->kbc/dot_general | solution.py:49
  349.2 42.6 %reduce-scatter.2.cloned.1.call-done = f32[1,96,768]{2,1,0:T(8,128)} async-done(((f32[1,768,768]{2,1,0:T(8,128)}), f32[1,96,768]{2,1,0:T(8,128)}) %reduce-scatter.2.cloned.1.call-update) | async-done | bytes 294928 | tf_op jit(solution)/shard_map/reduce_scatter | solution.py:50
  391.8 4.2 %fusion.17 = f32[1,96,768]{2,1,0:T(8,128)} fusion(f32[1,96,768]{2,1,0:T(8,128)} %reduce-scatter.2.cloned.1.call-done, f32[1,768,768]{2,1,0:T(8,128)} %all-gather.4.cloned.1.call-done, s32[]{:T(128)S(6)} %select_n.48), kind=kOutput, calls=%fused_computation.25 | convolution fusion | flops 679550976 | bytes 3342340 | tf_op jit(solution)/shard_map/kar,kac->krc/dot_general | solution.py:53
  (21 shorter events, 0.1 us)
Async XLA Ops:
  7.2 34.5 %copy-start = (f32[1,480,768]{2,1,0:T(8,128)S(1)}, f32[1,480,768]{2,1,0:T(8,128)}, u32[]{:S(2)}) copy-start(f32[1,480,768]{2,1,0:T(8,128)} %param.9) | copy-start | bytes 4423684
  7.2 42.8 %copy-start.5 = (s32[1,3840]{1,0:T(1,128)S(1)}, s32[1,3840]{1,0:T(1,128)}, u32[]{:S(2)}) copy-start(s32[1,3840]{1,0:T(1,128)} %param.11) | copy-start | bytes 46084
  7.2 34.5 %all-gather.4.cloned.1.call-start = ((), (), s32[]{:S(2)}) async-start(), calls=%async_computation.1 | async-start | bytes 2654208 | tf_op jit(solution)/shard_map/all_gather | solution.py:40
  7.9 307.8 %all-gather.6.cloned.1.call-start = ((), (), s32[]{:S(2)}) async-start(), calls=%async_computation.3 | async-start | bytes 13271040 | tf_op jit(solution)/shard_map/all_gather | solution.py:45
  48.2 343.6 %reduce-scatter.2.cloned.1.call-start = ((), (), s32[]{:S(2)}) async-start(), calls=%async_computation.2 | async-start | bytes 2654208 | tf_op jit(solution)/shard_map/reduce_scatter | solution.py:50
  48.4 205.5 %collective-permute-start = (f32[768,3072]{1,0:T(8,128)}, f32[768,3072]{1,0:T(8,128)}, u32[]{:S(2)}, u32[]{:S(2)}) collective-permute-start(f32[768,3072]{1,0:T(8,128)} %bitcast.36), channel_id=1, source_target_pairs={{0,8},{8,0},{16,24},{24,16},{1,9},{9,1},{17,25},{25,17},{2,10},{10... | collective-permute-start | bytes 28311560 | tf_op jit(solution)/shard_map/ppermute | solution.py:8
  308.9 4.5 %copy-start.2 = (f32[1920,480]{1,0:T(8,128)S(1)}, f32[1920,480]{1,0:T(8,128)}, u32[]{:S(2)}) copy-start(f32[1920,480]{1,0:T(8,128)} %gather_fusion.3) | copy-start | bytes 11059204
  315.7 27.9 %copy-start.3 = (f32[480,768]{1,0:T(8,128)S(1)}, f32[480,768]{1,0:T(8,128)}, u32[]{:S(2)}) copy-start(f32[480,768]{1,0:T(8,128)} %fusion.9) | copy-start | bytes 4423684
  342.5 1.1 copy-start.4
  343.6 52.5 %copy-start.1 = (f32[1,480,768]{2,1,0:T(8,128)S(1)}, f32[1,480,768]{2,1,0:T(8,128)}, u32[]{:S(2)}) copy-start(f32[1,480,768]{2,1,0:T(8,128)} %param.9) | copy-start | bytes 4423684
Sparse Core Ops, SparseCore 0:
  9.9 31.7 all-gather.3
  48.3 68.7 all-gather.5
  349.3 42.4 reduce-scatter.1
where the time goes:
time: 403 us
  waiting for transfers between devices  270 us (67%)
  local copies, waits for them, and re-layouts  55.7 us (14%)
  matrix products  43.1 us (11%)
  other arithmetic  18.3 us (5%)
  between operations  13.8 us (3%)
    ppermute x1, waiting for transfers between devices, partner(): lax.ppermute(x, axis, [(i, i ^ 1 << stride) for i in range(lax.axis_size(...  193 us
    reduce_scatter x1, waiting for transfers between devices, shards(): lax.psum_scatter(cross_terms, 'blk', scatter_dimension=1, tiled=True)  42.6 us
    gather x4, local copies, waits for them, and re-layouts, pick_panel(): return jnp.take(jnp.take(source, rows_here, axis=0), cols_here, axis=1)  41.5 us
    all_gather x1, waiting for transfers between devices, shards(): pivot_full = lax.all_gather(diag_inverse, 'blk', axis=1, tiled=True)  33.7 us
    dot_general x1, matrix products, shards(): jnp.einsum('rn,knb->krb', row_panel, lax.all_gather(factor, 'blk', axis=1...  26.8 us
    select_n x5, other arithmetic, pick_panel(): return jnp.take(jnp.take(source, rows_here, axis=0), cols_here, axis=1)  18.2 us
    select_n x2, local copies, waits for them, and re-layouts, pick_panel(): return jnp.take(jnp.take(source, rows_here, axis=0), cols_here, axis=1)  13 us
  transfers between devices with their start and end apart: 4, of which 3 were waited for; matrix products, arithmetic and copies ran while one was open for 18% of the time, Pallas kernels for 0%

commit v1 on v0

v1 whole, which is shorter than its diff:
```python
import functools

import jax
import jax.numpy as jnp
from jax import lax
from jax.experimental import pallas as pl
from jax.experimental.pallas import tpu as pltpu
from jax.sharding import PartitionSpec as P

F32, BF16 = jnp.float32, jnp.bfloat16
TOP = 3.3895313892515355e38
DOWN, UP = 1.0 / 64.0, 64.0
NN = (((1,), (0,)), ((), ()))
TN = (((0,), (0,)), ((), ()))
VMEM = pl.BlockSpec(memory_space=pltpu.VMEM)
SMEM = pl.BlockSpec(memory_space=pltpu.SMEM)


def split(x):
    high = jnp.clip(x, -TOP, TOP).astype(BF16)
    return high, (x - high.astype(F32)).astype(BF16)


def dot1(a, b, dims=NN):
    return lax.dot_general(a, b, dims, preferred_element_type=F32)


def dot3(a, b, dims=NN):
    return dot1(a[0], b[0], dims) + dot1(a[0], b[1], dims) + dot1(a[1], b[0], dims)


def params(**more):
    return pltpu.CompilerParams(vmem_limit_bytes=48 * 2**20, **more)


def pick_kernel(info, rows_ref, cols_ref, tile_ref, high_ref, low_ref):
    @pl.when(info[0] == 1)
    def _():
        height, width = tile_ref.shape
        picked = rows_ref.shape[0]
        at_row = lax.broadcasted_iota(jnp.int32, (picked, height), 1)
        row_hot = (at_row == rows_ref[...]).astype(F32).astype(BF16)
        high, low = split(tile_ref[...])
        high = dot1(row_hot, high).astype(BF16)
        low = dot1(row_hot, low).astype(BF16)
        at_col = lax.broadcasted_iota(jnp.int32, (width, picked), 0)
        for q in range(cols_ref.shape[0]):
            col_hot = (at_col == cols_ref[q]).astype(F32).astype(BF16)
            high_ref[q] = dot1(high, col_hot).astype(BF16)
            low_ref[q] = dot1(low, col_hot).astype(BF16)


def pick(active, tile, rows, cols, group):
    height, all_cols = tile.shape
    blocks, picked = cols.shape
    width = all_cols // blocks * group
    out = jax.ShapeDtypeStruct((blocks, picked, picked), BF16)
    return pl.pallas_call(
        pick_kernel,
        grid_spec=pltpu.PrefetchScalarGridSpec(
            num_scalar_prefetch=1,
            grid=(blocks // group,),
            in_specs=[
                pl.BlockSpec((picked, 1), lambda i, info: (0, 0)),
                pl.BlockSpec((group, 1, picked), lambda i, info: (i, 0, 0)),
                pl.BlockSpec((height, width), lambda i, info: (0, i * info[0])),
            ],
            out_specs=[pl.BlockSpec((group, picked, picked), lambda i, info: (i * info[0], 0, 0))] * 2,
        ),
        out_shape=[out, out],
        compiler_params=params(),
        name="pick",
    )(active[None], rows[:, None], cols[:, None, :], tile)


def apply_kernel(info, high_ref, low_ref, *refs):
    pieces, out_ref = refs[:-1], refs[-1]
    step = pl.program_id(0)

    @pl.when(info[0] == 1)
    def _():
        for p, piece in enumerate(pieces):

            @pl.when(step == p)
            def _(p=p, piece=piece):
                part = dot3((high_ref[0], low_ref[0]), split(piece[...] * DOWN))
                out_ref[...] = part if p == 0 else out_ref[...] + part


def apply(active, me, high, low, pieces):
    blocks, picked, _ = high.shape
    width = pieces[0].shape[1]
    block = pl.BlockSpec(
        (1, picked, picked), lambda p, info: (lax.bitwise_xor(info[1], p * info[0]), 0, 0)
    )
    whole = pl.BlockSpec((picked, width), lambda p, info: (0, 0))
    return pl.pallas_call(
        apply_kernel,
        grid_spec=pltpu.PrefetchScalarGridSpec(
            num_scalar_prefetch=1,
            grid=(blocks,),
            in_specs=[block, block] + [whole] * blocks,
            out_specs=whole,
        ),
        out_shape=jax.ShapeDtypeStruct((picked, width), F32),
        compiler_params=params(),
        cost_estimate=pl.CostEstimate(
            flops=6 * blocks * picked * picked * width,
            bytes_accessed=blocks * (4 * picked * picked + 4 * picked * width),
            transcendentals=0,
        ),
        name="apply",
    )(jnp.stack([active, me]), high, low, *pieces)


def back_kernel(info, high_ref, low_ref, lower_ref, *out_refs):
    step = pl.program_id(0)
    chunks = len(out_refs) // 2

    @pl.when(info[0] == 1)
    def _():
        width = lower_ref.shape[1] // chunks
        pair = (high_ref[0], low_ref[0])
        for c in range(chunks):
            rhs = split(lower_ref[:, c * width : (c + 1) * width] * DOWN)
            part = dot3(pair, rhs, TN)
            for parity in range(2):

                @pl.when(step % 2 == parity)
                def _(part=part, ref=out_refs[2 * c + parity]):
                    ref[0] = part


def back(active, me, high, low, lower, chunks):
    blocks, picked, _ = high.shape
    total = lower.shape[1]
    width = total // chunks
    block = pl.BlockSpec(
        (1, picked, picked), lambda p, info: (lax.bitwise_xor(info[1], p * info[0]), 0, 0)
    )
    out = jax.ShapeDtypeStruct((blocks // 2, picked, width), F32)
    flat = pl.pallas_call(
        back_kernel,
        grid_spec=pltpu.PrefetchScalarGridSpec(
            num_scalar_prefetch=1,
            grid=(blocks,),
            in_specs=[block, block, pl.BlockSpec((picked, total), lambda p, info: (0, 0))],
            out_specs=[pl.BlockSpec((1, picked, width), lambda p, info: (p // 2 * info[0], 0, 0))]
            * (2 * chunks),
        ),
        out_shape=[out] * (2 * chunks),
        compiler_params=params(),
        cost_estimate=pl.CostEstimate(
            flops=6 * blocks * picked * picked * total,
            bytes_accessed=blocks * (4 * picked * picked + 4 * picked * total),
            transcendentals=0,
        ),
        name="back",
    )(jnp.stack([active, me]), high, low, lower)
    return [(flat[2 * c], flat[2 * c + 1]) for c in range(chunks)]


def factor_kernel(lower_ref, pivot_ref, high_ref, low_ref):
    high_ref[...], low_ref[...] = split(dot3(split(lower_ref[...]), split(pivot_ref[...])))


def factor_of(lower, pivot):
    out = jax.ShapeDtypeStruct(lower.shape, BF16)
    return pl.pallas_call(
        factor_kernel,
        in_specs=[VMEM, VMEM],
        out_specs=[VMEM, VMEM],
        out_shape=[out, out],
        compiler_params=params(),
        cost_estimate=pl.CostEstimate(
            flops=6 * lower.size * lower.shape[1], bytes_accessed=8 * lower.size, transcendentals=0
        ),
        name="factor",
    )(lower, pivot)


def finish_kernel(chunk, first, info, *refs):
    here_ref, there_ref, arrived_ref, pivot_ref, high_ref, low_ref = refs[:6]
    earlier = refs[6 : 6 + chunk[1] - 1 - chunk[0]]
    rows_ref, sum_ref, keep_ref, send_ref, cross_ref = refs[-5:]
    width = here_ref.shape[1]
    at = chunk[0] * width
    mine = jnp.where(info[0] == 1, here_ref[...], there_ref[...]) + arrived_ref[...]
    sum_ref[...] = mine
    result = dot3(split(mine), split(pivot_ref[at : at + width, at : at + width]))
    for k, ref in enumerate(earlier):
        low_at = (chunk[0] + 1 + k) * width
        result += dot3(split(ref[...]), split(pivot_ref[low_at : low_at + width, at : at + width]))
    result = result * UP
    rows_ref[...] = -result
    cross_ref[...] = dot3((high_ref[...], low_ref[...]), split(result), TN)
    height = keep_ref.shape[1]
    for q in range(keep_ref.shape[0]):
        for parity, ref in enumerate((keep_ref, send_ref)):
            place = lax.bitwise_xor(info[1], 2 * q + parity)
            ref[q] = cross_ref[pl.ds(pl.multiple_of(place * height, 8), height), :]


def finish(chunk, count, same, blk, parts, here, there, arrived, pivot, factor, earlier, so_far):
    picked, width = here.shape
    order = pivot.shape[0]
    height = order // parts
    piece = jax.ShapeDtypeStruct((parts // 2, height, width), F32)
    operands = [jnp.stack([same, blk]), here, there, arrived, pivot, *factor, *earlier]
    in_specs = [SMEM] + [VMEM] * (len(operands) - 1)
    aliases = {}
    if so_far is not None:
        aliases = {len(operands): 0}
        operands.append(so_far)
        in_specs.append(pl.BlockSpec(memory_space=pl.ANY))
    return pl.pallas_call(
        functools.partial(finish_kernel, (chunk, count), so_far is None),
        grid=(1,),
        in_specs=in_specs,
        out_specs=[pl.BlockSpec((picked, width), lambda i: (0, chunk)), VMEM, VMEM, VMEM],
        out_shape=[
            jax.ShapeDtypeStruct((picked, order), F32),
            jax.ShapeDtypeStruct((picked, width), F32),
            piece,
            piece,
        ],
        scratch_shapes=[pltpu.VMEM((order, width), F32)],
        input_output_aliases=aliases,
        compiler_params=params(),
        cost_estimate=pl.CostEstimate(
            flops=6 * picked * width * (order + (1 + len(earlier)) * width),
            bytes_accessed=4 * (order * order + 4 * picked * width),
            transcendentals=0,
        ),
        name="finish",
    )(*operands)


def shards(ancestor_inv, lower_block, diag_inverse, row_index):
    grps, blks = lax.axis_size("grp"), lax.axis_size("blk")
    half = blks // 2
    tile, lower, names = ancestor_inv[0], lower_block[0], row_index[0]
    tile_rows, half_cols = tile.shape
    picked, order = lower.shape
    blk, grp = lax.axis_index("blk"), lax.axis_index("grp")
    side = grp % 2
    me = blk % half
    is_same = blk // half == side
    same = is_same.astype(jnp.int32)
    other = 1 - same
    one = jnp.ones((), jnp.int32)
    chunks = 3
    width = order // chunks

    everyone = [(g, b) for g in range(grps) for b in range(blks)]
    sames = [(g, b) for g, b in everyone if b // half == g % 2]
    others = [(g, b) for g, b in everyone if b // half != g % 2]

    def move(x, pairs):
        perm = [(g * blks + b, h * blks + c) for (g, b), (h, c) in pairs]
        return lax.ppermute(x, ("grp", "blk"), perm)

    def across(x, who, stride):
        return move(x, [((g, b), (g, b ^ stride)) for g, b in who])

    onward = [((g, b), (g, b ^ half)) for g, b in sames] + [((g, b), (g ^ 1, b)) for g, b in others]
    backward = [(to, at) for at, to in onward]

    def gather(x, who):
        pieces = {0: x}
        strides = [1 << s for s in range(1, half.bit_length() - 1)] + [1]
        for stride in strides:
            pieces.update({p ^ stride: across(piece, who, stride) for p, piece in list(pieces.items())})
        return [pieces[p] for p in range(half)]

    sibling_names = lax.ppermute(names, "grp", [(g, g ^ 1) for g in range(grps)])
    pivot = lax.all_gather(diag_inverse[0], "blk", axis=0, tiled=True)
    own_chunks = [lower[:, c * width : (c + 1) * width] for c in range(chunks)]
    order_of = list(range(chunks))[::-1]
    sent_on = {c: move(own_chunks[c], onward) for c in order_of}
    far = {c: gather(sent_on[c], everyone) for c in order_of}
    near = {c: gather(own_chunks[c], sames) for c in order_of}

    group = max(1, 768 // tile_rows)
    while half % group:
        group //= 2

    def lists(which):
        rows = lax.dynamic_slice_in_dim(which, blk * picked, picked) - blk * tile_rows
        cols = lax.dynamic_slice_in_dim(which, side * half * picked, half * picked)
        cols = cols.reshape(half, picked) - (side * half + jnp.arange(half)[:, None]) * tile_rows
        return rows, cols + (jnp.arange(half)[:, None] % group) * tile_rows

    own_pick = pick(same, tile, *lists(names), group)
    far_pick = pick(one, tile, *lists(jnp.where(is_same, sibling_names, names)), group)

    partial = back(other, me, *far_pick, lower, chunks)
    factor = factor_of(lower, pivot)

    earlier, so_far, crosses = [], None, {}
    for c in order_of:
        there = apply(one, me, *far_pick, far[c])
        keep, send = partial[c]
        left = keep + across(send, others, 1)
        for s in range(1, half.bit_length() - 1):
            stride = 1 << s
            left = left.reshape(left.shape[0] // 2, 2, picked, width)
            left = left[:, 0] + across(left[:, 1], others, stride)
        arrived = move(jnp.where(is_same, there, left[0]), backward)
        here = apply(same, me, *own_pick, near[c])
        so_far, total, keep, send = finish(
            c, chunks, same, blk, blks, here, there, arrived, pivot, factor, earlier, so_far
        )
        earlier = [total] + earlier
        left = keep + across(send, everyone, 1)
        crosses[c] = left[0] + sum(across(left[q], everyone, 2 * q) for q in range(1, half))

    cross = jnp.concatenate([crosses[c] for c in range(chunks)], axis=1)
    height = order // blks
    gram_cols = lax.dynamic_slice_in_dim(pivot, blk * height, height, 1)
    gram = jnp.einsum("ar,ac->rc", gram_cols, pivot, precision=lax.Precision.HIGHEST)
    return so_far[None], (gram + cross)[None]


def solution(mesh):
    in_specs = (P("grp", "blk", None), P("grp", "blk", None), P("grp", "blk", None), P("grp", None))
    out_specs = (P("grp", "blk", None), P("grp", "blk", None))
    return jax.shard_map(shards, mesh=mesh, in_specs=in_specs, out_specs=out_specs, check_vma=False)
```

time: 403 us -> 220 us (0.55)
  waiting for transfers between devices: 270 us -> 48.1 us
  Pallas kernels: 0 us -> 68.1 us
  starting transfers between devices: 1.85 us -> 61.1 us
  matrix products: 43.1 us -> 2.37 us
  local copies, waits for them, and re-layouts: 55.7 us -> 15.2 us
  other arithmetic: 18.3 us -> 9.2 us
    ppermute x1 -> x43, waiting for transfers between devices: 193 us -> 47.4 us  [the longest x42 47.4 us: move(): return lax.ppermute(x, ('grp', 'blk'), perm)]
    pallas_call x0 -> x13, Pallas kernels: none -> 68.1 us  [the longest x6 27.5 us: apply(): pl.pallas_call(apply_kernel, grid_spec=pltpu.PrefetchScalarGridSpec(num_s...]
    ppermute x1 -> x43, starting transfers between devices: 1.55 us -> 61 us  [the longest x42 57.9 us: move(): return lax.ppermute(x, ('grp', 'blk'), perm)]
    reduce_scatter x1 -> x0, waiting for transfers between devices: 42.6 us -> none  [shards(): lax.psum_scatter(cross_terms, 'blk', scatter_dimension=1, tiled=True)]
    gather x4 -> x0, local copies, waits for them, and re-layouts: 41.5 us -> none  [pick_panel(): return jnp.take(jnp.take(source, rows_here, axis=0), cols_here, axis=1)]
    dot_general x4 -> x1, matrix products: 43.1 us -> 2.37 us  [shards(): jnp.einsum('ar,ac->rc', gram_cols, pivot, precision=lax.Precision.HIGHEST)]
    all_gather x2 -> x1, waiting for transfers between devices: 33.7 us -> 0.02 us  [shards(): pivot = lax.all_gather(diag_inverse[0], 'blk', axis=0, tiled=True)]
    select_n x5 -> x4, other arithmetic: 18.2 us -> 3.67 us  [the longest x3 3.66 us: shards(): arrived = move(jnp.where(is_same, there, left[0]), backward)]
  transfers between devices with their start and end apart: 4 -> 44, of which waited for: 3 -> 12; matrix products, arithmetic and copies ran while one was open for 18% -> 6% of each run, Pallas kernels for 0% -> 29%
where the time goes in v1:
time: 220 us; the launch traced here: 219 us
  Pallas kernels  68.1 us (31%)
  starting transfers between devices  61.1 us (28%)
  waiting for transfers between devices  48.1 us (22%)
  local copies, waits for them, and re-layouts  15.2 us (7%)
  between operations  14.6 us (7%)
  other arithmetic  9.2 us (4%)
  matrix products  2.37 us (1%)
    ppermute x42, starting transfers between devices, move(): return lax.ppermute(x, ('grp', 'blk'), perm)  57.9 us
    ppermute x42, waiting for transfers between devices, move(): return lax.ppermute(x, ('grp', 'blk'), perm)  47.4 us
    pallas_call x6, Pallas kernels, apply(): pl.pallas_call(apply_kernel, grid_spec=pltpu.PrefetchScalarGridSpec(num_s...  27.5 us
    pallas_call x2, Pallas kernels, pick(): pl.pallas_call(pick_kernel, grid_spec=pltpu.PrefetchScalarGridSpec(num_sc...  21.3 us
    pallas_call x3, Pallas kernels, finish(): pl.pallas_call(functools.partial(finish_kernel, (chunk, count), so_far is...  13.9 us
    unnamed x40, local copies, waits for them, and re-layouts  12.3 us
  transfers between devices with their start and end apart: 44, of which 12 were waited for; matrix products, arithmetic and copies ran while one was open for 6% of the time, Pallas kernels for 29%

profile of v1, /device:TPU:0, one launch (start us, length us, event | category | flops | bytes accessed | tf_op | source)
XLA Modules:
  0.0 218.7 jit_solution(777775701505526119)
XLA Ops:
  8.7 3.1 %collective-permute-start.3 = (s32[3840]{0:T(1024)S(1)}, s32[3840]{0:T(1024)S(1)}, u32[]{:S(2)}, u32[]{:S(2)}) collective-permute-start(s32[3840]{0:T(1024)S(1)} %reduce.1), channel_id=1, source_target_pairs={{0,8},{8,0},{16,24},{24,16},{1,9},{9,1},{17,25},{25,17},{2,10},{10... | collective-permute-start | bytes 46088 | tf_op jit(solution)/shard_map/ppermute | solution.py:276
  13.2 3.4 %collective-permute-start.22 = (f32[480,256]{1,0:T(8,128)S(1)}, f32[480,256]{1,0:T(8,128)S(1)}, u32[]{:S(2)}, u32[]{:S(2)}) collective-permute-start(f32[480,256]{1,0:T(8,128)S(1)} %get-tuple-element.48.refs_0_), channel_id=1, source_target_pairs={{0,2},{1,3},{2,0},{3,1},{12,14},{13,15},{14,12},{15,13},{16,18},{1... | collective-permute-start | bytes 1474568 | tf_op jit(solution)/shard_map/ppermute | solution.py:261
  17.4 10.7 %pick.3 = (bf16[4,480,480]{2,1,0:T(8,128)(2,1)S(1)}, bf16[4,480,480]{2,1,0:T(8,128)(2,1)S(1)}) custom-call(s32[1]{0:T(128)} %constant.72.clone.1.info, s32[480,1]{1,0:T(8,128)S(1)} %copy.9.rows_ref, s32[4,1,480]{2,1,0:T(1,128)S(1)} %get-tuple-element.60.cols_ref, f32[768,3072]{1,0:T(8,128)} %bitcast.105), custom_call_target="tpu_custom_call" | custom-call | tf_op jit(solution)/shard_map/pick/pallas_call | solution.py:58
  30.6 3.4 %back.1 = (f32[2,480,256]{2,1,0:T(8,128)S(1)}, f32[2,480,256]{2,1,0:T(8,128)}, f32[2,480,256]{2,1,0:T(8,128)S(1)}, f32[2,480,256]{2,1,0:T(8,128)}, f32[2,480,256]{2,1,0:T(8,128)S(1)}, /*index=5*/f32[2,480,256]{2,1,0:T(8,128)}) custom-call(s32[2]{0:T(128)S(1)} %pad_add_fusion.2.info, bf16[4,480,480]{2,1,0:T(8,128)(2,1)} %copy-done.3, ...), custom_call_target="tpu_custom_call" | custom-call | flops 4246732800 | bytes 9584640 | tf_op jit(solution)/shard_map/back/pallas_call | solution.py:142
  43.5 8.2 %collective-permute-start.24 = (f32[480,256]{1,0:T(8,128)S(1)}, f32[480,256]{1,0:T(8,128)}, u32[]{:S(2)}, u32[]{:S(2)}) collective-permute-start(f32[480,256]{1,0:T(8,128)S(1)} %get-tuple-element.48.refs_0_), channel_id=1, source_target_pairs={{0,4},{1,5},{2,6},{3,7},{12,8},{13,9},{14,10},{15,11},{16,20},{17,... | collective-permute-start | bytes 1474568 | tf_op jit(solution)/shard_map/ppermute | solution.py:261
  54.9 10.7 %pick.2 = (bf16[4,480,480]{2,1,0:T(8,128)(2,1)S(1)}, bf16[4,480,480]{2,1,0:T(8,128)(2,1)S(1)}) custom-call(s32[1]{0:T(128)} %bitcast.info, s32[480,1]{1,0:T(8,128)S(1)} %copy.8.rows_ref, s32[4,1,480]{2,1,0:T(1,128)S(1)} %get-tuple-element.61.cols_ref, f32[768,3072]{1,0:T(8,128)} %bitcast.106), custom_call_target="tpu_custom_call" | custom-call | tf_op jit(solution)/shard_map/pick/pallas_call | solution.py:58
  68.0 4.6 %apply.10.refs_0_ = f32[480,256]{1,0:T(8,128)S(1)} custom-call(s32[2]{0:T(128)S(1)} %pad_add_fusion.3.info, bf16[4,480,480]{2,1,0:T(8,128)(2,1)S(1)} %get-tuple-element.25.high_ref, bf16[4,480,480]{2,1,0:T(8,128)(2,1)} %copy-done.2, f32[480,256]{1,0:T(8,128)S(1)} %get-tuple-element.48.refs_0_, f32[480,256]{1,0:T(8,128)S(1)} %copy-done.14, ...), custom_call_target="tpu_custom_call" | custom-call | flops 1415577600 | bytes 5652480 | tf_op jit(solution)/shard_map/apply/pallas_call | solution.py:97
  77.7 8.4 %collective-permute-done.4.refs_0_ = f32[480,256]{1,0:T(8,128)S(1)} collective-permute-done((f32[480,256]{1,0:T(8,128)S(1)}, f32[480,256]{1,0:T(8,128)S(1)}, u32[]{:S(2)}, u32[]{:S(2)}) %collective-permute-start.4) | collective-permute-done | bytes 491552 | tf_op jit(solution)/shard_map/ppermute | solution.py:261
  90.5 7.1 %collective-permute-done.16.refs_2_ = f32[480,256]{1,0:T(8,128)S(1)} collective-permute-done((f32[480,256]{1,0:T(8,128)S(1)}, f32[480,256]{1,0:T(8,128)S(1)}, u32[]{:S(2)}, u32[]{:S(2)}) %collective-permute-start.16) | collective-permute-done | bytes 491552 | tf_op jit(solution)/shard_map/ppermute | solution.py:261
  97.6 9.8 %collective-permute-done.6.refs_2_ = f32[480,256]{1,0:T(8,128)S(1)} collective-permute-done((f32[480,256]{1,0:T(8,128)S(1)}, f32[480,256]{1,0:T(8,128)S(1)}, u32[]{:S(2)}, u32[]{:S(2)}) %collective-permute-start.6) | collective-permute-done | bytes 491552 | tf_op jit(solution)/shard_map/ppermute | solution.py:261
  109.7 4.6 %apply.11.refs_1_ = f32[480,256]{1,0:T(8,128)S(1)} custom-call(s32[2]{0:T(128)S(1)} %pad_add_fusion.1.info, bf16[4,480,480]{2,1,0:T(8,128)(2,1)S(1)} %copy-done.4, bf16[4,480,480]{2,1,0:T(8,128)(2,1)} %copy-done.5, f32[480,256]{1,0:T(8,128)} %collective-permute-done.24.refs_0_, f32[480,256]{1,0:T(8,128)S(1)} %collective-permute-done.25.refs_1_, ...), custom_call_target="tpu_custom_call" | custom-call | flops 1415577600 | bytes 5652480 | tf_op jit(solution)/shard_map/apply/pallas_call | solution.py:97
  114.3 3.4 %collective-permute-start.12 = (f32[480,256]{1,0:T(8,128)S(1)}, f32[480,256]{1,0:T(8,128)S(1)}, u32[]{:S(2)}, u32[]{:S(2)}) collective-permute-start(f32[480,256]{1,0:T(8,128)S(1)} %get-tuple-element.49.refs_0_), channel_id=1, source_target_pairs={{0,2},{1,3},{2,0},{3,1},{12,14},{13,15},{14,12},{15,13},{16,18},{1... | collective-permute-start | bytes 1474568 | tf_op jit(solution)/shard_map/ppermute | solution.py:261
  117.8 2.4 %collective-permute-start.1 = (f32[480,256]{1,0:T(8,128)S(1)}, f32[480,256]{1,0:T(8,128)S(1)}, u32[]{:S(2)}, u32[]{:S(2)}) collective-permute-start(f32[480,256]{1,0:T(8,128)S(1)} %get-tuple-element.50.refs_0_), channel_id=1, source_target_pairs={{0,2},{1,3},{2,0},{3,1},{12,14},{13,15},{14,12},{15,13},{16,18},{1... | collective-permute-start | bytes 1474568 | tf_op jit(solution)/shard_map/ppermute | solution.py:261
  121.1 4.5 %apply.9.refs_1_ = f32[480,256]{1,0:T(8,128)S(1)} custom-call(s32[2]{0:T(128)S(1)} %pad_add_fusion.1.info, bf16[4,480,480]{2,1,0:T(8,128)(2,1)S(1)} %copy-done.4, bf16[4,480,480]{2,1,0:T(8,128)(2,1)} %copy-done.5, f32[480,256]{1,0:T(8,128)S(1)} %collective-permute-done.14.refs_0_, f32[480,256]{1,0:T(8,128)S(1)} %collective-permute-done.15.refs_1_, ...), custom_call_target="tpu_custom_call" | custom-call | flops 1415577600 | bytes 5652480 | tf_op jit(solution)/shard_map/apply/pallas_call | solution.py:97
  127.5 4.5 %apply.7.refs_1_ = f32[480,256]{1,0:T(8,128)S(1)} custom-call(s32[2]{0:T(128)S(1)} %pad_add_fusion.1.info, bf16[4,480,480]{2,1,0:T(8,128)(2,1)S(1)} %copy-done.4, bf16[4,480,480]{2,1,0:T(8,128)(2,1)} %copy-done.5, f32[480,256]{1,0:T(8,128)S(1)} %collective-permute-done.4.refs_0_, f32[480,256]{1,0:T(8,128)S(1)} %collective-permute-done.5.refs_1_, ...), custom_call_target="tpu_custom_call" | custom-call | flops 1415577600 | bytes 5652480 | tf_op jit(solution)/shard_map/apply/pallas_call | solution.py:97
  137.1 3.3 %collective-permute-done.1.refs_2_ = f32[480,256]{1,0:T(8,128)S(1)} collective-permute-done((f32[480,256]{1,0:T(8,128)S(1)}, f32[480,256]{1,0:T(8,128)S(1)}, u32[]{:S(2)}, u32[]{:S(2)}) %collective-permute-start.1) | collective-permute-done | bytes 491552 | tf_op jit(solution)/shard_map/ppermute | solution.py:261
  149.4 4.5 %apply.8.refs_0_ = f32[480,256]{1,0:T(8,128)S(1)} custom-call(s32[2]{0:T(128)S(1)} %pad_add_fusion.3.info, bf16[4,480,480]{2,1,0:T(8,128)(2,1)S(1)} %get-tuple-element.25.high_ref, bf16[4,480,480]{2,1,0:T(8,128)(2,1)} %copy-done.2, f32[480,256]{1,0:T(8,128)S(1)} %get-tuple-element.49.refs_0_, f32[480,256]{1,0:T(8,128)S(1)} %collective-permute-done.11.refs_1_, ...), custom_call_target="tpu_custom_call" | custom-call | flops 1415577600 | bytes 5652480 | tf_op jit(solution)/shard_map/apply/pallas_call | solution.py:97
  154.0 4.7 %apply.6.refs_0_ = f32[480,256]{1,0:T(8,128)S(1)} custom-call(s32[2]{0:T(128)S(1)} %pad_add_fusion.3.info, bf16[4,480,480]{2,1,0:T(8,128)(2,1)S(1)} %get-tuple-element.25.high_ref, bf16[4,480,480]{2,1,0:T(8,128)(2,1)} %copy-done.2, f32[480,256]{1,0:T(8,128)S(1)} %get-tuple-element.50.refs_0_, f32[480,256]{1,0:T(8,128)S(1)} %collective-permute-done.refs_1_, ...), custom_call_target="tpu_custom_call" | custom-call | flops 1415577600 | bytes 5652480 | tf_op jit(solution)/shard_map/apply/pallas_call | solution.py:97
  163.8 3.9 %finish.3 = (f32[480,768]{1,0:T(8,128)}, f32[480,256]{1,0:T(8,128)S(1)}, f32[4,96,256]{2,1,0:T(8,128)S(1)}, f32[4,96,256]{2,1,0:T(8,128)S(1)}) custom-call(s32[2]{0:T(128)S(1)} %pad_add_fusion.info, f32[480,256]{1,0:T(8,128)S(1)} %apply.10.refs_0_, f32[480,256]{1,0:T(8,128)S(1)} %apply.11.refs_1_, f32[480,256]{1,0:T(8,128)} %collective-permute-done.30.refs_2_, ...), custom_call_target="tpu_custom_call" | custom-call | flops 754974720 | bytes 4325376 | tf_op jit(solution)/shard_map/finish/pallas_call | solution.py:216
  169.2 11.0 %collective-permute-done.20.refs_2_ = f32[480,256]{1,0:T(8,128)} collective-permute-done((f32[480,256]{1,0:T(8,128)}, f32[480,256]{1,0:T(8,128)}, u32[]{:S(2)}, u32[]{:S(2)}) %collective-permute-start.20) | collective-permute-done | bytes 491552 | tf_op jit(solution)/shard_map/ppermute | solution.py:261
  180.1 4.7 %finish.4 = (f32[480,768]{1,0:T(8,128)}, f32[480,256]{1,0:T(8,128)S(1)}, f32[4,96,256]{2,1,0:T(8,128)S(1)}, f32[4,96,256]{2,1,0:T(8,128)}) custom-call(s32[2]{0:T(128)S(1)} %pad_add_fusion.info, f32[480,256]{1,0:T(8,128)S(1)} %apply.8.refs_0_, f32[480,256]{1,0:T(8,128)S(1)} %apply.9.refs_1_, ...), custom_call_target="tpu_custom_call", output_to_operand_aliasing={{0}: (8, {})} | custom-call | flops 943718400 | bytes 4325376 | tf_op jit(solution)/shard_map/finish/pallas_call | solution.py:216
  184.9 5.3 %finish.5 = (f32[480,768]{1,0:T(8,128)}, f32[480,256]{1,0:T(8,128)}, f32[4,96,256]{2,1,0:T(8,128)S(1)}, f32[4,96,256]{2,1,0:T(8,128)}) custom-call(s32[2]{0:T(128)S(1)} %pad_add_fusion.info, f32[480,256]{1,0:T(8,128)S(1)} %apply.6.refs_0_, f32[480,256]{1,0:T(8,128)S(1)} %apply.7.refs_1_, ...), custom_call_target="tpu_custom_call", output_to_operand_aliasing={{0}: (9, {})} | custom-call | flops 1132462080 | bytes 4325376 | tf_op jit(solution)/shard_map/finish/pallas_call | solution.py:216
  192.4 2.9 %collective-permute-start.34 = (f32[96,256]{1,0:T(8,128)S(1)}, f32[96,256]{1,0:T(8,128)S(1)}, u32[]{:S(2)}, u32[]{:S(2)}) collective-permute-start(f32[96,256]{1,0:T(8,128)S(1)} %get-tuple-element.52), channel_id=1, source_target_pairs={{0,6},{1,7},{2,4},{3,5},{4,2},{5,3},{6,0},{7,1},{8,14},{9,15},{10,... | collective-permute-start | bytes 294920 | tf_op jit(solution)/shard_map/ppermute | solution.py:261
  196.0 2.9 %collective-permute-start.38 = (f32[96,256]{1,0:T(8,128)S(1)}, f32[96,256]{1,0:T(8,128)S(1)}, u32[]{:S(2)}, u32[]{:S(2)}) collective-permute-start(f32[96,256]{1,0:T(8,128)S(1)} %get-tuple-element.55), channel_id=1, source_target_pairs={{0,6},{1,7},{2,4},{3,5},{4,2},{5,3},{6,0},{7,1},{8,14},{9,15},{10,... | collective-permute-start | bytes 294920 | tf_op jit(solution)/shard_map/ppermute | solution.py:261
  (154 shorter events, 72.3 us)
Async XLA Ops:
  7.2 151.5 %all-gather.3.cloned.1.call-start = ((), (), s32[]{:S(2)}) async-start(), calls=%async_computation | async-start | bytes 2654208 | tf_op jit(solution)/shard_map/all_gather | solution.py:277
  13.2 26.3 %collective-permute-start.22 = (f32[480,256]{1,0:T(8,128)S(1)}, f32[480,256]{1,0:T(8,128)S(1)}, u32[]{:S(2)}, u32[]{:S(2)}) collective-permute-start(f32[480,256]{1,0:T(8,128)S(1)} %get-tuple-element.48.refs_0_), channel_id=1, source_target_pairs={{0,2},{1,3},{2,0},{3,1},{12,14},{13,15},{14,12},{15,13},{16,18},{1... | collective-permute-start | bytes 1474568 | tf_op jit(solution)/shard_map/ppermute | solution.py:261
  36.0 36.8 %collective-permute-start.8 = (f32[2,480,256]{2,1,0:T(8,128)}, f32[2,480,256]{2,1,0:T(8,128)}, u32[]{:S(2)}, u32[]{:S(2)}) collective-permute-start(f32[2,480,256]{2,1,0:T(8,128)} %get-tuple-element.30), channel_id=1, source_target_pairs={{4,5},{5,4},{6,7},{7,6},{8,9},{9,8},{10,11},{11,10},{20,21},{21,20... | collective-permute-start | bytes 2949128 | tf_op jit(solution)/shard_map/ppermute | solution.py:261
  39.5 15.0 %collective-permute-start.23 = (f32[480,256]{1,0:T(8,128)S(1)}, f32[480,256]{1,0:T(8,128)}, u32[]{:S(2)}, u32[]{:S(2)}) collective-permute-start(f32[480,256]{1,0:T(8,128)S(1)} %collective-permute-done.22.refs_2_), channel_id=1, source_target_pairs={{0,1},{1,0},{2,3},{3,2},{12,13},{13,12},{14,15},{15,14},{16,17},{1... | collective-permute-start | bytes 1474568 | tf_op jit(solution)/shard_map/ppermute | solution.py:261
  41.9 33.8 %collective-permute-start.18 = (f32[2,480,256]{2,1,0:T(8,128)}, f32[2,480,256]{2,1,0:T(8,128)}, u32[]{:S(2)}, u32[]{:S(2)}) collective-permute-start(f32[2,480,256]{2,1,0:T(8,128)} %get-tuple-element.34), channel_id=1, source_target_pairs={{4,5},{5,4},{6,7},{7,6},{8,9},{9,8},{10,11},{11,10},{20,21},{21,20... | collective-permute-start | bytes 2949128 | tf_op jit(solution)/shard_map/ppermute | solution.py:261
  43.5 29.1 %collective-permute-start.24 = (f32[480,256]{1,0:T(8,128)S(1)}, f32[480,256]{1,0:T(8,128)}, u32[]{:S(2)}, u32[]{:S(2)}) collective-permute-start(f32[480,256]{1,0:T(8,128)S(1)} %get-tuple-element.48.refs_0_), channel_id=1, source_target_pairs={{0,4},{1,5},{2,6},{3,7},{12,8},{13,9},{14,10},{15,11},{16,20},{17,... | collective-permute-start | bytes 1474568 | tf_op jit(solution)/shard_map/ppermute | solution.py:261
  52.6 36.0 %collective-permute-start.28 = (f32[2,480,256]{2,1,0:T(8,128)}, f32[2,480,256]{2,1,0:T(8,128)}, u32[]{:S(2)}, u32[]{:S(2)}) collective-permute-start(f32[2,480,256]{2,1,0:T(8,128)} %get-tuple-element.36), channel_id=1, source_target_pairs={{4,5},{5,4},{6,7},{7,6},{8,9},{9,8},{10,11},{11,10},{20,21},{21,20... | collective-permute-start | bytes 2949128 | tf_op jit(solution)/shard_map/ppermute | solution.py:261
  54.5 21.1 %collective-permute-start.14 = (f32[480,256]{1,0:T(8,128)S(1)}, f32[480,256]{1,0:T(8,128)S(1)}, u32[]{:S(2)}, u32[]{:S(2)}) collective-permute-start(f32[480,256]{1,0:T(8,128)S(1)} %get-tuple-element.49.refs_0_), channel_id=1, source_target_pairs={{0,4},{1,5},{2,6},{3,7},{12,8},{13,9},{14,10},{15,11},{16,20},{17,... | collective-permute-start | bytes 1474568 | tf_op jit(solution)/shard_map/ppermute | solution.py:261
  75.7 21.9 %collective-permute-start.16 = (f32[480,256]{1,0:T(8,128)S(1)}, f32[480,256]{1,0:T(8,128)S(1)}, u32[]{:S(2)}, u32[]{:S(2)}) collective-permute-start(f32[480,256]{1,0:T(8,128)S(1)} %collective-permute-done.14.refs_0_), channel_id=1, source_target_pairs={{0,2},{1,3},{2,0},{3,1},{4,6},{5,7},{6,4},{7,5},{8,10},{9,11},{10,... | collective-permute-start | bytes 1474568 | tf_op jit(solution)/shard_map/ppermute | solution.py:261
  86.0 28.3 %collective-permute-start.15 = (f32[480,256]{1,0:T(8,128)S(1)}, f32[480,256]{1,0:T(8,128)S(1)}, u32[]{:S(2)}, u32[]{:S(2)}) collective-permute-start(f32[480,256]{1,0:T(8,128)S(1)} %collective-permute-done.14.refs_0_), channel_id=1, source_target_pairs={{0,1},{1,0},{2,3},{3,2},{4,5},{5,4},{6,7},{7,6},{8,9},{9,8},{10,11... | collective-permute-start | bytes 1474568 | tf_op jit(solution)/shard_map/ppermute | solution.py:261
  87.1 20.4 %collective-permute-start.6 = (f32[480,256]{1,0:T(8,128)S(1)}, f32[480,256]{1,0:T(8,128)S(1)}, u32[]{:S(2)}, u32[]{:S(2)}) collective-permute-start(f32[480,256]{1,0:T(8,128)S(1)} %collective-permute-done.4.refs_0_), channel_id=1, source_target_pairs={{0,2},{1,3},{2,0},{3,1},{4,6},{5,7},{6,4},{7,5},{8,10},{9,11},{10,... | collective-permute-start | bytes 1474568 | tf_op jit(solution)/shard_map/ppermute | solution.py:261
  88.6 18.9 %collective-permute-start.27 = (f32[480,256]{1,0:T(8,128)S(1)}, f32[480,256]{1,0:T(8,128)S(1)}, u32[]{:S(2)}, u32[]{:S(2)}) collective-permute-start(f32[480,256]{1,0:T(8,128)S(1)} %collective-permute-done.26.refs_2_), channel_id=1, source_target_pairs={{0,1},{1,0},{2,3},{3,2},{4,5},{5,4},{6,7},{7,6},{8,9},{9,8},{10,11... | collective-permute-start | bytes 1474568 | tf_op jit(solution)/shard_map/ppermute | solution.py:261
  90.0 27.8 %collective-permute-start.5 = (f32[480,256]{1,0:T(8,128)S(1)}, f32[480,256]{1,0:T(8,128)S(1)}, u32[]{:S(2)}, u32[]{:S(2)}) collective-permute-start(f32[480,256]{1,0:T(8,128)S(1)} %collective-permute-done.4.refs_0_), channel_id=1, source_target_pairs={{0,1},{1,0},{2,3},{3,2},{4,5},{5,4},{6,7},{7,6},{8,9},{9,8},{10,11... | collective-permute-start | bytes 1474568 | tf_op jit(solution)/shard_map/ppermute | solution.py:261
  97.6 22.6 %collective-permute-start.17 = (f32[480,256]{1,0:T(8,128)S(1)}, f32[480,256]{1,0:T(8,128)S(1)}, u32[]{:S(2)}, u32[]{:S(2)}) collective-permute-start(f32[480,256]{1,0:T(8,128)S(1)} %collective-permute-done.16.refs_2_), channel_id=1, source_target_pairs={{0,1},{1,0},{2,3},{3,2},{4,5},{5,4},{6,7},{7,6},{8,9},{9,8},{10,11... | collective-permute-start | bytes 1474568 | tf_op jit(solution)/shard_map/ppermute | solution.py:261
  107.4 18.2 %collective-permute-start.7 = (f32[480,256]{1,0:T(8,128)S(1)}, f32[480,256]{1,0:T(8,128)S(1)}, u32[]{:S(2)}, u32[]{:S(2)}) collective-permute-start(f32[480,256]{1,0:T(8,128)S(1)} %collective-permute-done.6.refs_2_), channel_id=1, source_target_pairs={{0,1},{1,0},{2,3},{3,2},{4,5},{5,4},{6,7},{7,6},{8,9},{9,8},{10,11... | collective-permute-start | bytes 1474568 | tf_op jit(solution)/shard_map/ppermute | solution.py:261
  107.4 24.6 %collective-permute-start.9 = (f32[1,480,256]{2,1,0:T(8,128)S(1)}, f32[1,480,256]{2,1,0:T(8,128)}, u32[]{:S(2)}, u32[]{:S(2)}) collective-permute-start(f32[1,480,256]{2,1,0:T(8,128)S(1)} %slice_bitcast_fusion.4), channel_id=1, source_target_pairs={{4,6},{5,7},{6,4},{7,5},{8,10},{9,11},{10,8},{11,9},{20,22},{21,23... | collective-permute-start | bytes 1474568 | tf_op jit(solution)/shard_map/ppermute | solution.py:261
  114.3 20.3 %collective-permute-start.12 = (f32[480,256]{1,0:T(8,128)S(1)}, f32[480,256]{1,0:T(8,128)S(1)}, u32[]{:S(2)}, u32[]{:S(2)}) collective-permute-start(f32[480,256]{1,0:T(8,128)S(1)} %get-tuple-element.49.refs_0_), channel_id=1, source_target_pairs={{0,2},{1,3},{2,0},{3,1},{12,14},{13,15},{14,12},{15,13},{16,18},{1... | collective-permute-start | bytes 1474568 | tf_op jit(solution)/shard_map/ppermute | solution.py:261
  117.8 22.6 %collective-permute-start.1 = (f32[480,256]{1,0:T(8,128)S(1)}, f32[480,256]{1,0:T(8,128)S(1)}, u32[]{:S(2)}, u32[]{:S(2)}) collective-permute-start(f32[480,256]{1,0:T(8,128)S(1)} %get-tuple-element.50.refs_0_), channel_id=1, source_target_pairs={{0,2},{1,3},{2,0},{3,1},{12,14},{13,15},{14,12},{15,13},{16,18},{1... | collective-permute-start | bytes 1474568 | tf_op jit(solution)/shard_map/ppermute | solution.py:261
  120.2 22.1 %collective-permute-start.29 = (f32[1,480,256]{2,1,0:T(8,128)}, f32[1,480,256]{2,1,0:T(8,128)S(1)}, u32[]{:S(2)}, u32[]{:S(2)}) collective-permute-start(f32[1,480,256]{2,1,0:T(8,128)} %slice_bitcast_fusion), channel_id=1, source_target_pairs={{4,6},{5,7},{6,4},{7,5},{8,10},{9,11},{10,8},{11,9},{20,22},{21,23... | collective-permute-start | bytes 1474568 | tf_op jit(solution)/shard_map/ppermute | solution.py:261
  125.6 22.0 %collective-permute-start.11 = (f32[480,256]{1,0:T(8,128)S(1)}, f32[480,256]{1,0:T(8,128)S(1)}, u32[]{:S(2)}, u32[]{:S(2)}) collective-permute-start(f32[480,256]{1,0:T(8,128)S(1)} %get-tuple-element.49.refs_0_), channel_id=1, source_target_pairs={{0,1},{1,0},{2,3},{3,2},{12,13},{13,12},{14,15},{15,14},{16,17},{1... | collective-permute-start | bytes 1474568 | tf_op jit(solution)/shard_map/ppermute | solution.py:261
  134.7 19.3 %collective-permute-start = (f32[480,256]{1,0:T(8,128)S(1)}, f32[480,256]{1,0:T(8,128)S(1)}, u32[]{:S(2)}, u32[]{:S(2)}) collective-permute-start(f32[480,256]{1,0:T(8,128)S(1)} %get-tuple-element.50.refs_0_), channel_id=1, source_target_pairs={{0,1},{1,0},{2,3},{3,2},{12,13},{13,12},{14,15},{15,14},{16,17},{1... | collective-permute-start | bytes 1474568 | tf_op jit(solution)/shard_map/ppermute | solution.py:261
  145.6 18.1 %collective-permute-start.30 = (f32[480,256]{1,0:T(8,128)}, f32[480,256]{1,0:T(8,128)}, u32[]{:S(2)}, u32[]{:S(2)}) collective-permute-start(f32[480,256]{1,0:T(8,128)} %fusion.2), channel_id=1, source_target_pairs={{4,0},{5,1},{6,2},{7,3},{8,12},{9,13},{10,14},{11,15},{20,16},{21,... | collective-permute-start | bytes 1474568 | tf_op jit(solution)/shard_map/ppermute | solution.py:261
  147.6 37.3 %collective-permute-start.10 = (f32[480,256]{1,0:T(8,128)}, f32[480,256]{1,0:T(8,128)}, u32[]{:S(2)}, u32[]{:S(2)}) collective-permute-start(f32[480,256]{1,0:T(8,128)} %fusion.8), channel_id=1, source_target_pairs={{4,0},{5,1},{6,2},{7,3},{8,12},{9,13},{10,14},{11,15},{20,16},{21,... | collective-permute-start | bytes 1474568 | tf_op jit(solution)/shard_map/ppermute | solution.py:261
  148.4 31.8 %collective-permute-start.20 = (f32[480,256]{1,0:T(8,128)}, f32[480,256]{1,0:T(8,128)}, u32[]{:S(2)}, u32[]{:S(2)}) collective-permute-start(f32[480,256]{1,0:T(8,128)} %fusion.5), channel_id=1, source_target_pairs={{4,0},{5,1},{6,2},{7,3},{8,12},{9,13},{10,14},{11,15},{20,16},{21,... | collective-permute-start | bytes 1474568 | tf_op jit(solution)/shard_map/ppermute | solution.py:261
  (40 other events, 293.5 us)
Sparse Core Ops, SparseCore 0:
  9.9 34.8 all-gather.2

commit v2 on v1

v2 whole, which is shorter than its diff:
```python
import functools

import jax
import jax.numpy as jnp
from jax import lax
from jax.experimental import pallas as pl
from jax.experimental.pallas import tpu as pltpu
from jax.sharding import PartitionSpec as P

F32, BF16 = jnp.float32, jnp.bfloat16
TOP = 3.3895313892515355e38
COST = 3.3e6
DOWN, UP = 1.0 / 64.0, 64.0
NN = (((1,), (0,)), ((), ()))
VMEM = pl.BlockSpec(memory_space=pltpu.VMEM)
ANY = pl.BlockSpec(memory_space=pl.ANY)
HBM = pl.BlockSpec(memory_space=pltpu.HBM)
SMEM = pl.BlockSpec(memory_space=pltpu.SMEM)


def split(x):
    high = jnp.clip(x, -TOP, TOP).astype(BF16)
    return high, (x - high.astype(F32)).astype(BF16)


def dot1(a, b, dims=NN):
    return lax.dot_general(a, b, dims, preferred_element_type=F32)


def dot3(a, b, dims=NN):
    return dot1(a[0], b[0], dims) + dot1(a[0], b[1], dims) + dot1(a[1], b[0], dims)


def wide3(high, low, rhs):
    width = rhs[0].shape[1]
    pair = dot1(high, jnp.concatenate(rhs, axis=1))
    return pair[:, :width] + pair[:, width:] + dot1(low, rhs[0])


def cost(microseconds):
    return pl.CostEstimate(
        flops=0, bytes_accessed=int(microseconds * COST), transcendentals=0
    )


def params(mib):
    return pltpu.CompilerParams(vmem_limit_bytes=mib * 2**20)


def load_tile(tile_ref, slots, sems, step, steps):
    width = slots.shape[2]

    def copy(at):
        slot = at % 2
        source = tile_ref.at[:, pl.ds(pl.multiple_of(at * width, 128), width)]
        return pltpu.make_async_copy(source, slots.at[slot], sems.at[slot])

    @pl.when(step == 0)
    def _():
        copy(step).start()

    @pl.when(step + 1 < steps)
    def _():
        copy(step + 1).start()

    copy(step).wait()
    return slots[step % 2]


def hot_rows(rows_ref, hot_ref):
    at_row = lax.broadcasted_iota(jnp.int32, hot_ref.shape, 1)
    hot_ref[...] = (at_row == rows_ref[...]).astype(F32).astype(BF16)


def pick_block(block, cols_ref, hot_ref, high_ref, low_ref):
    picked = hot_ref.shape[0]
    pair = split(block)
    both = jnp.concatenate([dot1(hot_ref[...], piece) for piece in pair], axis=0).astype(BF16)
    at_col = lax.broadcasted_iota(jnp.int32, (block.shape[1], picked), 0)
    for q in range(cols_ref.shape[0]):
        col_hot = (at_col == cols_ref[q]).astype(F32).astype(BF16)
        result = dot1(both, col_hot)
        high_ref[q] = result[:picked].astype(BF16)
        low_ref[q] = result[picked:].astype(BF16)


def pick_kernel(rows_ref, cols_ref, tile_ref, high_ref, low_ref, hot_ref, slots, sems):
    step = pl.program_id(0)

    @pl.when(step == 0)
    def _():
        hot_rows(rows_ref, hot_ref)

    block = load_tile(tile_ref, slots, sems, step, pl.num_programs(0))
    pick_block(block, cols_ref, hot_ref, high_ref, low_ref)


def pick(tile, rows, cols, group):
    height, all_cols = tile.shape
    blocks, picked = cols.shape
    width = all_cols // blocks * group
    out = jax.ShapeDtypeStruct((blocks, picked, picked), BF16)
    return pl.pallas_call(
        pick_kernel,
        grid=(blocks // group,),
        in_specs=[
            pl.BlockSpec((picked, 1), lambda i: (0, 0)),
            pl.BlockSpec((group, 1, picked), lambda i: (i, 0, 0)),
            HBM,
        ],
        out_specs=[pl.BlockSpec((group, picked, picked), lambda i: (i, 0, 0))] * 2,
        scratch_shapes=[
            pltpu.VMEM((picked, height), BF16),
            pltpu.VMEM((2, height, width), F32),
            pltpu.SemaphoreType.DMA((2,)),
        ],
        out_shape=[out] * 2,
        compiler_params=params(56),
        cost_estimate=cost(10),
        name="pick",
    )(rows[:, None], cols[:, None, :], tile)


def second_kernel(steps, info, rows_ref, cols_ref, tile_ref, q_high, q_low, lower_ref, *refs):
    high_ref, low_ref = refs[:2]
    hot_ref, slots, sems, lower_high, lower_low = refs[-5:]
    out_refs = refs[2:-5]
    chunks = len(out_refs) // 2
    width = lower_ref.shape[1] // chunks
    step = pl.program_id(0)

    @pl.when((info[0] == 1) & (step == 0))
    def _():
        hot_rows(rows_ref, hot_ref)

    @pl.when((info[0] == 1) & (step < steps))
    def _():
        block = load_tile(tile_ref, slots, sems, step, steps)
        pick_block(block, cols_ref, hot_ref, high_ref, low_ref)

    @pl.when((info[0] == 0) & (step == 0))
    def _():
        lower_high[...], lower_low[...] = split(lower_ref[...] * DOWN)

    @pl.when(info[0] == 0)
    def _():
        high, low = jnp.transpose(q_high[0]), jnp.transpose(q_low[0])
        full = dot1(high, lower_high[...]) + dot1(high, lower_low[...]) + dot1(low, lower_high[...])
        for parity in range(2):

            @pl.when(step % 2 == parity)
            def _(parity=parity):
                for c in range(chunks):
                    out_refs[2 * c + parity][0] = full[:, c * width : (c + 1) * width]


def second(same, me, tile, rows, cols, group, high, low, lower, chunks):
    height, all_cols = tile.shape
    blocks, picked = cols.shape
    total = lower.shape[1]
    width = all_cols // blocks * group
    steps = blocks // group
    out = jax.ShapeDtypeStruct((blocks, picked, picked), BF16)
    back = jax.ShapeDtypeStruct((blocks // 2, picked, total // chunks), F32)

    def at_pick(p, info):
        return (jnp.minimum(p, steps - 1) * info[0], 0, 0)

    def at_block(p, info):
        return (lax.bitwise_xor(info[1], p * (1 - info[0])), 0, 0)

    def at_back(p, info):
        return (p // 2 * (1 - info[0]), 0, 0)

    flat = pl.pallas_call(
        functools.partial(second_kernel, steps),
        grid_spec=pltpu.PrefetchScalarGridSpec(
            num_scalar_prefetch=1,
            grid=(blocks,),
            in_specs=[
                pl.BlockSpec((picked, 1), lambda p, info: (0, 0)),
                pl.BlockSpec((group, 1, picked), at_pick),
                HBM,
                pl.BlockSpec((1, picked, picked), at_block),
                pl.BlockSpec((1, picked, picked), at_block),
                pl.BlockSpec((picked, total), lambda p, info: (0, 0)),
            ],
            out_specs=[pl.BlockSpec((group, picked, picked), at_pick)] * 2
            + [pl.BlockSpec((1, picked, total // chunks), at_back)] * (2 * chunks),
            scratch_shapes=[
                pltpu.VMEM((picked, height), BF16),
                pltpu.VMEM((2, height, width), F32),
                pltpu.SemaphoreType.DMA((2,)),
            ]
            + [pltpu.VMEM((picked, total), BF16)] * 2,
        ),
        out_shape=[out] * 2 + [back] * (2 * chunks),
        compiler_params=params(56),
        cost_estimate=cost(10),
        name="second",
    )(jnp.stack([same, me]), rows[:, None], cols[:, None, :], tile, high, low, lower)
    return flat[:2], [(flat[2 + 2 * c], flat[3 + 2 * c]) for c in range(chunks)]


def apply_kernel(info, high_ref, low_ref, *refs):
    pieces, out_ref = refs[:-1], refs[-1]
    step = pl.program_id(0)

    @pl.when(info[0] == 1)
    def _():
        for p, piece in enumerate(pieces):

            @pl.when(step == p)
            def _(p=p, piece=piece):
                part = wide3(high_ref[0], low_ref[0], split(piece[...] * DOWN))
                out_ref[...] = part if p == 0 else out_ref[...] + part


def apply(active, me, high, low, pieces):
    blocks, picked, _ = high.shape
    width = pieces[0].shape[1]
    block = pl.BlockSpec(
        (1, picked, picked), lambda p, info: (lax.bitwise_xor(info[1], p * info[0]), 0, 0)
    )
    whole = pl.BlockSpec((picked, width), lambda p, info: (0, 0))
    return pl.pallas_call(
        apply_kernel,
        grid_spec=pltpu.PrefetchScalarGridSpec(
            num_scalar_prefetch=1,
            grid=(blocks,),
            in_specs=[block, block] + [whole] * blocks,
            out_specs=whole,
        ),
        out_shape=jax.ShapeDtypeStruct((picked, width), F32),
        compiler_params=params(12),
        cost_estimate=cost(4.5),
        name="apply",
    )(jnp.stack([active, me]), high, low, *pieces)


def factor_kernel(lower_ref, pivot_ref, high_ref, low_ref):
    full = dot3(split(lower_ref[...]), split(pivot_ref[...]))
    high_ref[...], low_ref[...] = split(jnp.transpose(full))


def factor_of(lower, pivot):
    out = jax.ShapeDtypeStruct(lower.shape[::-1], BF16)
    return pl.pallas_call(
        factor_kernel,
        in_specs=[VMEM, VMEM],
        out_specs=[VMEM, VMEM],
        out_shape=[out, out],
        compiler_params=params(16),
        cost_estimate=cost(2.2),
        name="factor",
    )(lower, pivot)


def finish_kernel(chunk, count, info, *refs):
    local_ref, arrived_ref, pivot_ref, high_ref, low_ref = refs[:5]
    earlier = refs[5 : 5 + count - 1 - chunk]
    rows_ref, sum_ref, keep_ref, send_ref, cross_ref = refs[-5:]
    width = local_ref.shape[1]
    at = chunk * width
    mine = local_ref[...] + arrived_ref[...]
    sum_ref[...] = mine
    result = dot3(split(mine), split(pivot_ref[at : at + width, at : at + width]))
    for k, ref in enumerate(earlier):
        low_at = (chunk + 1 + k) * width
        result += dot3(split(ref[...]), split(pivot_ref[low_at : low_at + width, at : at + width]))
    result = result * UP
    rows_ref[...] = -result
    cross_ref[...] = dot3((high_ref[...], low_ref[...]), split(result))
    height = keep_ref.shape[1]
    for q in range(keep_ref.shape[0]):
        for parity, ref in enumerate((keep_ref, send_ref)):
            place = lax.bitwise_xor(info[0], 2 * q + parity)
            ref[q] = cross_ref[pl.ds(pl.multiple_of(place * height, 8), height), :]


def finish(chunk, count, blk, parts, local, arrived, pivot, factor, earlier, so_far):
    picked, width = local.shape
    order = pivot.shape[0]
    height = order // parts
    piece = jax.ShapeDtypeStruct((parts // 2, height, width), F32)
    operands = [blk[None], local, arrived, pivot, *factor, *earlier]
    in_specs = [SMEM] + [VMEM] * (len(operands) - 1)
    aliases = {}
    if so_far is not None:
        aliases = {len(operands): 0}
        operands.append(so_far)
        in_specs.append(ANY)
    return pl.pallas_call(
        functools.partial(finish_kernel, chunk, count),
        grid=(1,),
        in_specs=in_specs,
        out_specs=[pl.BlockSpec((picked, width), lambda i: (0, chunk)), VMEM, VMEM, VMEM],
        out_shape=[
            jax.ShapeDtypeStruct((picked, order), F32),
            jax.ShapeDtypeStruct((picked, width), F32),
            piece,
            piece,
        ],
        scratch_shapes=[pltpu.VMEM((order, width), F32)],
        input_output_aliases=aliases,
        compiler_params=params(20),
        cost_estimate=cost(5),
        name="finish",
    )(*operands)


def shards(ancestor_inv, lower_block, diag_inverse, row_index):
    grps, blks = lax.axis_size("grp"), lax.axis_size("blk")
    half = blks // 2
    tile, lower, names = ancestor_inv[0], lower_block[0], row_index[0]
    tile_rows, half_cols = tile.shape
    picked, order = lower.shape
    blk, grp = lax.axis_index("blk"), lax.axis_index("grp")
    side = grp % 2
    me = blk % half
    is_same = blk // half == side
    same = is_same.astype(jnp.int32)
    one = jnp.ones((), jnp.int32)
    chunks = 2
    width = order // chunks

    everyone = [(g, b) for g in range(grps) for b in range(blks)]
    sames = [(g, b) for g, b in everyone if b // half == g % 2]
    others = [(g, b) for g, b in everyone if b // half != g % 2]

    def move(x, pairs):
        perm = [(g * blks + b, h * blks + c) for (g, b), (h, c) in pairs]
        return lax.ppermute(x, ("grp", "blk"), perm)

    def across(x, who, stride):
        return move(x, [((g, b), (g, b ^ stride)) for g, b in who])

    def after(*arrays):
        return lax.optimization_barrier(arrays)

    onward = [((g, b), (g, b ^ half)) for g, b in sames] + [((g, b), (g ^ 1, b)) for g, b in others]
    backward = [(to, at) for at, to in onward]

    def on_core(x, who=everyone):
        return across(x, who, 1)

    def spread(arrays, who):
        arrays.update({p ^ 1: on_core(x, who) for p, x in list(arrays.items())})
        return [arrays[p] for p in range(half)]

    chips = [2 * s for s in range(half // 2)]

    def chip_gather(x, who):
        return {0: x} | {p: across(x, who, p) for p in chips[1:]}

    own = lax.optimization_barrier([lower[:, c * width : (c + 1) * width] for c in range(chunks)])
    high, low = chunks - 1, 0
    sent = {c: move(own[c], onward) for c in (high, low)}
    near = {high: chip_gather(own[high], sames)}
    sibling_names = lax.ppermute(names, "grp", [(g, g ^ 1) for g in range(grps)])
    pivot = lax.all_gather(diag_inverse[0], "blk", axis=0, tiled=True)

    group = max(1, 768 // tile_rows)
    while half % group:
        group //= 2

    def lists(which):
        rows = lax.dynamic_slice_in_dim(which, blk * picked, picked) - blk * tile_rows
        cols = lax.dynamic_slice_in_dim(which, side * half * picked, half * picked)
        cols = cols.reshape(half, picked) - (side * half + jnp.arange(half)[:, None]) * tile_rows
        return rows, cols + (jnp.arange(half)[:, None] % group) * tile_rows

    own_pick = pick(tile, *lists(names), group)
    sibling_names, own_pick, sent[high] = after(sibling_names, own_pick, sent[high])
    sib_pick, partial = second(
        same, me, tile, *lists(sibling_names), group, *own_pick, lower, chunks
    )

    def sum_cores(keep, send):
        got = on_core(send, others)
        return {i: keep[i] + got[i] for i in range(half // 2)}

    def sum_chips(places):
        for s in range(half.bit_length() - 2):
            for i in [i for i in places if i >> s & 1]:
                places[i ^ 1 << s] += across(places.pop(i), others, 2 << s)
        return places[0]

    sib_high = chip_gather(sent[high], sames)
    partial[high], sib_high, near[high], sent[low] = after(
        partial[high], sib_high, near[high], sent[low]
    )
    partial[low], sent[low] = after(partial[low], sent[low])
    sums = {c: sum_cores(*partial[c]) for c in (high, low)}
    away = {c: {i: x for i, x in sums[c].items() if i} for c in sums}
    away, sib_high = after(away, sib_high)
    back_sum = {c: sum_chips(away[c] | {0: sums[c][0]}) for c in (high, low)}
    sib = {high: spread(sib_high, sames)}
    sib_low = chip_gather(sent[low], sames)

    passed = {p: across(x, sames, half) for p, x in near[high].items() if p}
    high_parts = {p: jnp.where(is_same, x, passed[p]) if p else jnp.where(is_same, x, sent[high]) for p, x in near[high].items()}
    low_parts = chip_gather(jnp.where(is_same, own[low], sent[low]), everyone)

    result = apply(same, me, *sib_pick, sib[high])
    arrived = {high: move(jnp.where(is_same, result, back_sum[high]), backward)}
    result, sib_low = after(result, sib_low)
    sib[low], back_sum[low] = after(spread(sib_low, sames), back_sum[low])
    result = apply(same, me, *sib_pick, sib[low])
    arrived[low] = move(jnp.where(is_same, result, back_sum[low]), backward)

    result, high_parts, pivot = after(result, high_parts, pivot)

    height = order // blks
    gram_cols = lax.dynamic_slice_in_dim(pivot, blk * height, height, 1)
    gram = jnp.einsum("ar,ac->rc", gram_cols, pivot, precision=lax.Precision.HIGHEST)
    factor = factor_of(lower, pivot)
    local = apply(one, me, *own_pick, spread(high_parts, everyone))
    factor, gram, local = after(factor, gram, local)
    so_far, total, keep, send = finish(
        high, chunks, blk, blks, local, arrived[high], pivot, factor, [], None
    )

    def scatter(keep, send):
        left = keep + on_core(send)
        return left[0] + sum(across(left[q], everyone, 2 * q) for q in range(1, half))

    crosses = {high: scatter(keep, send)}
    total, low_parts = after(total, low_parts)
    local = apply(one, me, *own_pick, spread(low_parts, everyone))
    so_far, _, keep, send = finish(
        low, chunks, blk, blks, local, arrived[low], pivot, factor, [total], so_far
    )
    crosses[low] = scatter(keep, send)

    cross = jnp.concatenate([crosses[c] for c in range(chunks)], axis=1)
    return so_far[None], (gram + cross)[None]


def solution(mesh):
    in_specs = (P("grp", "blk", None), P("grp", "blk", None), P("grp", "blk", None), P("grp", None))
    out_specs = (P("grp", "blk", None), P("grp", "blk", None))
    return jax.shard_map(shards, mesh=mesh, in_specs=in_specs, out_specs=out_specs, check_vma=False)
```

time: 220 us -> 168 us (0.76)
  starting transfers between devices: 61.1 us -> 40.5 us
  waiting for transfers between devices: 48.1 us -> 35.1 us
  Pallas kernels: 68.1 us -> 56.4 us
  local copies, waits for them, and re-layouts: 15.2 us -> 6.97 us
  other arithmetic: 9.2 us -> 11.8 us
    ppermute x42 -> x29, starting transfers between devices: 57.9 us -> 40.4 us  [move(): return lax.ppermute(x, ('grp', 'blk'), perm)]
    ppermute x42 -> x29, waiting for transfers between devices: 47.4 us -> 35.1 us  [move(): return lax.ppermute(x, ('grp', 'blk'), perm)]
    unnamed x40 -> x32, local copies, waits for them, and re-layouts: 12.3 us -> 2.64 us
    pallas_call x6 -> x4, Pallas kernels: 27.5 us -> 19.1 us  [apply(): pl.pallas_call(apply_kernel, grid_spec=pltpu.PrefetchScalarGridSpec(num_s...]
    reshape x3 -> x0, other arithmetic: 3.99 us -> none  [shards(): left = left.reshape(left.shape[0] // 2, 2, picked, width)]
    pallas_call x6 -> x4, Pallas kernels: 38.6 us -> 35.1 us  [the longest x1 15.2 us: second(): pl.pallas_call(functools.partial(second_kernel, steps), grid_spec=pltpu.P...]
    ppermute x1, starting transfers between devices: 3.09 us -> 0.07 us  [shards(): lax.ppermute(names, 'grp', [(g, g ^ 1) for g in range(grps)])]
    select_n x4 -> x5, other arithmetic: 3.67 us -> 6.41 us  [the longest x1 2.08 us: shards(): low_parts = chip_gather(jnp.where(is_same, own[low], sent[low]), everyone)]
  transfers between devices with their start and end apart: 44 -> 31, of which waited for: 12 -> 10; matrix products, arithmetic and copies ran while one was open for 6% -> 9% of each run, Pallas kernels for 29% -> 34%
where the time goes in v2:
time: 168 us; the launch traced here: 167 us
  Pallas kernels  56.4 us (34%)
  starting transfers between devices  40.5 us (24%)
  waiting for transfers between devices  35.1 us (21%)
  between operations  14.6 us (9%)
  other arithmetic  11.8 us (7%)
  local copies, waits for them, and re-layouts  6.97 us (4%)
    ppermute x29, starting transfers between devices, move(): return lax.ppermute(x, ('grp', 'blk'), perm)  40.4 us
    ppermute x29, waiting for transfers between devices, move(): return lax.ppermute(x, ('grp', 'blk'), perm)  35.1 us
    pallas_call x4, Pallas kernels, apply(): pl.pallas_call(apply_kernel, grid_spec=pltpu.PrefetchScalarGridSpec(num_s...  19.1 us
    pallas_call x1, Pallas kernels, second(): pl.pallas_call(functools.partial(second_kernel, steps), grid_spec=pltpu.P...  15.2 us
    pallas_call x1, Pallas kernels, pick(): pl.pallas_call(pick_kernel, grid=(blocks // group,), in_specs=[pl.BlockSp...  12 us
    pallas_call x2, Pallas kernels, finish(): pl.pallas_call(functools.partial(finish_kernel, chunk, count), grid=(1,),...  7.95 us
  transfers between devices with their start and end apart: 31, of which 10 were waited for; matrix products, arithmetic and copies ran while one was open for 9% of the time, Pallas kernels for 34%

profile of v2, /device:TPU:0, one launch (start us, length us, event | category | flops | bytes accessed | tf_op | source)
XLA Modules:
  0.0 166.9 jit_solution(17432838119940616989)
XLA Ops:
  7.2 2.3 %fusion.13 = (f32[480,384]{1,0:T(8,128)}, f32[480,384]{1,0:T(8,128)S(1)}) fusion(f32[480,768]{1,0:T(8,128)} %bitcast.51), kind=kLoop, calls=%fused_computation.38 | loop fusion | bytes 2949120 | tf_op jit(solution)/shard_map/slice | solution.py:356
  9.5 3.0 %collective-permute-start.1 = (f32[480,384]{1,0:T(8,128)}, f32[480,384]{1,0:T(8,128)S(1)}, u32[]{:S(2)}, u32[]{:S(2)}) collective-permute-start(f32[480,384]{1,0:T(8,128)} %get-tuple-element.87), channel_id=1, source_target_pairs={{0,4},{1,5},{2,6},{3,7},{12,8},{13,9},{14,10},{15,11},{16,20},{17,... | collective-permute-start | bytes 2211848 | tf_op jit(solution)/shard_map/ppermute | solution.py:333
  12.5 3.4 %collective-permute-start.3 = (f32[480,384]{1,0:T(8,128)}, f32[480,384]{1,0:T(8,128)}, u32[]{:S(2)}, u32[]{:S(2)}) collective-permute-start(f32[480,384]{1,0:T(8,128)} %get-tuple-element.87), channel_id=1, source_target_pairs={{0,2},{1,3},{2,0},{3,1},{12,14},{13,15},{14,12},{15,13},{16,18},{1... | collective-permute-start | bytes 2211848 | tf_op jit(solution)/shard_map/ppermute | solution.py:333
  16.0 2.1 %collective-permute-start.4 = (f32[480,384]{1,0:T(8,128)S(1)}, f32[480,384]{1,0:T(8,128)S(1)}, u32[]{:S(2)}, u32[]{:S(2)}) collective-permute-start(f32[480,384]{1,0:T(8,128)S(1)} %get-tuple-element.69), channel_id=1, source_target_pairs={{0,4},{1,5},{2,6},{3,7},{12,8},{13,9},{14,10},{15,11},{16,20},{17,... | collective-permute-start | bytes 2211848 | tf_op jit(solution)/shard_map/ppermute | solution.py:333
  19.8 12.0 %pick.1 = (bf16[4,480,480]{2,1,0:T(8,128)(2,1)}, bf16[4,480,480]{2,1,0:T(8,128)(2,1)}) custom-call(s32[480,1]{1,0:T(8,128)} %copy.7.rows_ref, s32[4,1,480]{2,1,0:T(1,128)} %broadcast_subtract_fusion.1.cols_ref, f32[768,3072]{1,0:T(8,128)} %bitcast.54), custom_call_target="tpu_custom_call" | custom-call | bytes 33000000 | tf_op jit(solution)/shard_map/pick/pallas_call | solution.py:103
  31.8 2.5 %collective-permute-start.2 = (f32[480,384]{1,0:T(8,128)S(1)}, f32[480,384]{1,0:T(8,128)S(1)}, u32[]{:S(2)}, u32[]{:S(2)}) collective-permute-start(f32[480,384]{1,0:T(8,128)S(1)} %collective-permute-done.1.refs_0_), channel_id=1, source_target_pairs={{0,2},{1,3},{2,0},{3,1},{12,14},{13,15},{14,12},{15,13},{16,18},{1... | collective-permute-start | bytes 2211848 | tf_op jit(solution)/shard_map/ppermute | solution.py:333
  36.7 15.2 %second.1 = (bf16[4,480,480]{2,1,0:T(8,128)(2,1)}, bf16[4,480,480]{2,1,0:T(8,128)(2,1)}, f32[2,480,384]{2,1,0:T(8,128)}, f32[2,480,384]{2,1,0:T(8,128)}, f32[2,480,384]{2,1,0:T(8,128)}, /*index=5*/f32[2,480,384]{2,1,0:T(8,128)}) custom-call(s32[2]{0:T(128)} %pad_add_fusion.1.info, s32[480,1]{1,0:T(8,128)} %copy.8.rows_ref, ...), custom_call_target="tpu_custom_call" | custom-call | bytes 33000000 | tf_op jit(solution)/shard_map/second/pallas_call | solution.py:175
  56.8 2.2 %collective-permute-start.7 = (f32[480,384]{1,0:T(8,128)S(1)}, f32[480,384]{1,0:T(8,128)S(1)}, u32[]{:S(2)}, u32[]{:S(2)}) collective-permute-start(f32[480,384]{1,0:T(8,128)S(1)} %collective-permute-done.1.refs_0_), channel_id=1, source_target_pairs={{0,1},{1,0},{2,3},{3,2},{12,13},{13,12},{14,15},{15,14},{16,17},{1... | collective-permute-start | bytes 2211848 | tf_op jit(solution)/shard_map/ppermute | solution.py:333
  59.0 2.4 %collective-permute-start.8 = (f32[480,384]{1,0:T(8,128)S(1)}, f32[480,384]{1,0:T(8,128)S(1)}, u32[]{:S(2)}, u32[]{:S(2)}) collective-permute-start(f32[480,384]{1,0:T(8,128)S(1)} %collective-permute-done.2.refs_2_), channel_id=1, source_target_pairs={{0,1},{1,0},{2,3},{3,2},{12,13},{13,12},{14,15},{15,14},{16,17},{1... | collective-permute-start | bytes 2211848 | tf_op jit(solution)/shard_map/ppermute | solution.py:333
  61.4 2.4 %collective-permute-start.9 = (f32[480,384]{1,0:T(8,128)S(1)}, f32[480,384]{1,0:T(8,128)S(1)}, u32[]{:S(2)}, u32[]{:S(2)}) collective-permute-start(f32[480,384]{1,0:T(8,128)S(1)} %collective-permute-done.4.refs_0_), channel_id=1, source_target_pairs={{0,2},{1,3},{2,0},{3,1},{12,14},{13,15},{14,12},{15,13},{16,18},{1... | collective-permute-start | bytes 2211848 | tf_op jit(solution)/shard_map/ppermute | solution.py:333
  67.9 4.1 %apply.4 = f32[480,384]{1,0:T(8,128)S(1)} custom-call(s32[2]{0:T(128)S(1)} %copy-done.10, bf16[4,480,480]{2,1,0:T(8,128)(2,1)S(1)} %copy-done.5, bf16[4,480,480]{2,1,0:T(8,128)(2,1)S(1)} %copy-done.6, f32[480,384]{1,0:T(8,128)S(1)} %collective-permute-done.1.refs_0_, f32[480,384]{1,0:T(8,128)S(1)} %collective-permute-done.7.refs_1_, ...), custom_call_target="tpu_custom_call" | custom-call | bytes 14850000 | tf_op jit(solution)/shard_map/apply/pallas_call | solution.py:226
  72.0 9.7 %collective-permute-done.9.refs_2_ = f32[480,384]{1,0:T(8,128)S(1)} collective-permute-done((f32[480,384]{1,0:T(8,128)S(1)}, f32[480,384]{1,0:T(8,128)S(1)}, u32[]{:S(2)}, u32[]{:S(2)}) %collective-permute-start.9) | collective-permute-done | bytes 737312 | tf_op jit(solution)/shard_map/ppermute | solution.py:333
  83.7 2.4 %collective-permute-start.11 = (f32[480,384]{1,0:T(8,128)S(1)}, f32[480,384]{1,0:T(8,128)S(1)}, u32[]{:S(2)}, u32[]{:S(2)}) collective-permute-start(f32[480,384]{1,0:T(8,128)S(1)} %collective-permute-done.9.refs_2_), channel_id=1, source_target_pairs={{0,1},{1,0},{2,3},{3,2},{12,13},{13,12},{14,15},{15,14},{16,17},{1... | collective-permute-start | bytes 2211848 | tf_op jit(solution)/shard_map/ppermute | solution.py:333
  90.1 4.1 %apply.5 = f32[480,384]{1,0:T(8,128)S(1)} custom-call(s32[2]{0:T(128)S(1)} %copy-done.10, bf16[4,480,480]{2,1,0:T(8,128)(2,1)S(1)} %copy-done.5, bf16[4,480,480]{2,1,0:T(8,128)(2,1)S(1)} %copy-done.6, f32[480,384]{1,0:T(8,128)S(1)} %collective-permute-done.4.refs_0_, f32[480,384]{1,0:T(8,128)S(1)} %collective-permute-done.10.refs_1_, ...), custom_call_target="tpu_custom_call" | custom-call | bytes 14850000 | tf_op jit(solution)/shard_map/apply/pallas_call | solution.py:226
  95.7 2.1 %broadcast_select_fusion.1.refs_0_ = f32[480,384]{1,0:T(8,128)} fusion(f32[480,384]{1,0:T(8,128)} %copy-done.11, f32[480,384]{1,0:T(8,128)S(1)} %collective-permute-done.4.refs_0_, pred[]{:T(512)S(6)} %eq.9), kind=kLoop, calls=%fused_computation.14 | loop fusion | flops 184320 | bytes 2211841 | tf_op jit(solution)/shard_map/jit(_where)/select_n | solution.py:403
  100.0 2.2 %factor.1 = (bf16[768,480]{1,0:T(8,128)(2,1)S(1)}, bf16[768,480]{1,0:T(8,128)(2,1)S(1)}) custom-call(f32[480,768]{1,0:T(8,128)S(1)} %bitcast.53, f32[768,768]{1,0:T(8,128)S(1)} %bitcast.47), custom_call_target="tpu_custom_call" | custom-call | bytes 7260000 | tf_op jit(solution)/shard_map/factor/pallas_call | solution.py:248
  103.9 5.5 %apply.6.refs_0_ = f32[480,384]{1,0:T(8,128)S(1)} custom-call(s32[2]{0:T(128)S(1)} %pad_add_fusion.info, bf16[4,480,480]{2,1,0:T(8,128)(2,1)S(1)} %copy-done.2, bf16[4,480,480]{2,1,0:T(8,128)(2,1)S(1)} %copy-done.3, f32[480,384]{1,0:T(8,128)S(1)} %broadcast_select_fusion.3.refs_0_, f32[480,384]{1,0:T(8,128)} %collective-permute-done.14.refs_1_, ...), custom_call_target="tpu_custom_call" | custom-call | bytes 14850000 | tf_op jit(solution)/shard_map/apply/pallas_call | solution.py:226
  109.4 4.2 %finish.2 = (f32[480,768]{1,0:T(8,128)}, f32[480,384]{1,0:T(8,128)S(1)}, f32[4,96,384]{2,1,0:T(8,128)S(1)}, f32[4,96,384]{2,1,0:T(8,128)S(1)}) custom-call(s32[1]{0:T(128)} %bitcast.info, f32[480,384]{1,0:T(8,128)S(1)} %apply.6.refs_0_, f32[480,384]{1,0:T(8,128)} %collective-permute-done.17.refs_1_, f32[768,768]{1,0:T(8,128)S(1)} %bitcast.49, ...), custom_call_target="tpu_custom_call" | custom-call | bytes 16500000 | tf_op jit(solution)/shard_map/finish/pallas_call | solution.py:293
  113.6 2.9 %collective-permute-done.18.refs_2_ = f32[480,384]{1,0:T(8,128)} collective-permute-done((f32[480,384]{1,0:T(8,128)}, f32[480,384]{1,0:T(8,128)}, u32[]{:S(2)}, u32[]{:S(2)}) %collective-permute-start.18) | collective-permute-done | bytes 737312 | tf_op jit(solution)/shard_map/ppermute | solution.py:333
  117.1 4.6 %collective-permute-start.21 = (f32[480,384]{1,0:T(8,128)S(1)}, f32[480,384]{1,0:T(8,128)S(1)}, u32[]{:S(2)}, u32[]{:S(2)}) collective-permute-start(f32[480,384]{1,0:T(8,128)S(1)} %broadcast_select_fusion), channel_id=1, source_target_pairs={{4,0},{5,1},{6,2},{7,3},{8,12},{9,13},{10,14},{11,15},{20,16},{21,... | collective-permute-start | bytes 2211848 | tf_op jit(solution)/shard_map/ppermute | solution.py:333
  121.7 5.4 %apply.7.refs_0_ = f32[480,384]{1,0:T(8,128)S(1)} custom-call(s32[2]{0:T(128)S(1)} %pad_add_fusion.info, bf16[4,480,480]{2,1,0:T(8,128)(2,1)S(1)} %copy-done.2, bf16[4,480,480]{2,1,0:T(8,128)(2,1)S(1)} %copy-done.3, f32[480,384]{1,0:T(8,128)} %broadcast_select_fusion.1.refs_0_, f32[480,384]{1,0:T(8,128)S(1)} %collective-permute-done.19.refs_1_, ...), custom_call_target="tpu_custom_call" | custom-call | bytes 14850000 | tf_op jit(solution)/shard_map/apply/pallas_call | solution.py:226
  127.1 11.2 %collective-permute-done.21.refs_1_ = f32[480,384]{1,0:T(8,128)S(1)} collective-permute-done((f32[480,384]{1,0:T(8,128)S(1)}, f32[480,384]{1,0:T(8,128)S(1)}, u32[]{:S(2)}, u32[]{:S(2)}) %collective-permute-start.21) | collective-permute-done | bytes 737312 | tf_op jit(solution)/shard_map/ppermute | solution.py:333
  138.4 3.8 %finish.3 = (f32[480,768]{1,0:T(8,128)}, f32[480,384]{1,0:T(8,128)}, f32[4,96,384]{2,1,0:T(8,128)S(1)}, f32[4,96,384]{2,1,0:T(8,128)S(1)}) custom-call(s32[1]{0:T(128)} %bitcast.info, f32[480,384]{1,0:T(8,128)S(1)} %apply.7.refs_0_, f32[480,384]{1,0:T(8,128)S(1)} %collective-permute-done.21.refs_1_, ...), custom_call_target="tpu_custom_call", output_to_operand_aliasing={{0}: (7, {})} | custom-call | bytes 16500000 | tf_op jit(solution)/shard_map/finish/pallas_call | solution.py:293
  155.3 2.3 %collective-permute-done.24 = f32[96,384]{1,0:T(8,128)S(1)} collective-permute-done((f32[96,384]{1,0:T(8,128)S(1)}, f32[96,384]{1,0:T(8,128)S(1)}, u32[]{:S(2)}, u32[]{:S(2)}) %collective-permute-start.24) | collective-permute-done | bytes 147488 | tf_op jit(solution)/shard_map/ppermute | solution.py:333
  (111 shorter events, 40.5 us)
Async XLA Ops:
  7.2 88.0 %all-gather.3.cloned.1.call-start = ((), (), s32[]{:S(2)}) async-start(), calls=%async_computation | async-start | bytes 2654208 | tf_op jit(solution)/shard_map/all_gather | solution.py:361
  9.5 22.3 %collective-permute-start.1 = (f32[480,384]{1,0:T(8,128)}, f32[480,384]{1,0:T(8,128)S(1)}, u32[]{:S(2)}, u32[]{:S(2)}) collective-permute-start(f32[480,384]{1,0:T(8,128)} %get-tuple-element.87), channel_id=1, source_target_pairs={{0,4},{1,5},{2,6},{3,7},{12,8},{13,9},{14,10},{15,11},{16,20},{17,... | collective-permute-start | bytes 2211848 | tf_op jit(solution)/shard_map/ppermute | solution.py:333
  12.5 39.4 %collective-permute-start.3 = (f32[480,384]{1,0:T(8,128)}, f32[480,384]{1,0:T(8,128)}, u32[]{:S(2)}, u32[]{:S(2)}) collective-permute-start(f32[480,384]{1,0:T(8,128)} %get-tuple-element.87), channel_id=1, source_target_pairs={{0,2},{1,3},{2,0},{3,1},{12,14},{13,15},{14,12},{15,13},{16,18},{1... | collective-permute-start | bytes 2211848 | tf_op jit(solution)/shard_map/ppermute | solution.py:333
  16.0 15.8 %collective-permute-start = (s32[3840]{0:T(1024)S(1)}, s32[3840]{0:T(1024)S(1)}, u32[]{:S(2)}, u32[]{:S(2)}) collective-permute-start(s32[3840]{0:T(1024)S(1)} %reduce), channel_id=1, source_target_pairs={{0,8},{8,0},{16,24},{24,16},{1,9},{9,1},{17,25},{25,17},{2,10},{10... | collective-permute-start | bytes 46088 | tf_op jit(solution)/shard_map/ppermute | solution.py:360
  16.0 35.9 %collective-permute-start.4 = (f32[480,384]{1,0:T(8,128)S(1)}, f32[480,384]{1,0:T(8,128)S(1)}, u32[]{:S(2)}, u32[]{:S(2)}) collective-permute-start(f32[480,384]{1,0:T(8,128)S(1)} %get-tuple-element.69), channel_id=1, source_target_pairs={{0,4},{1,5},{2,6},{3,7},{12,8},{13,9},{14,10},{15,11},{16,20},{17,... | collective-permute-start | bytes 2211848 | tf_op jit(solution)/shard_map/ppermute | solution.py:333
  31.8 22.2 %collective-permute-start.2 = (f32[480,384]{1,0:T(8,128)S(1)}, f32[480,384]{1,0:T(8,128)S(1)}, u32[]{:S(2)}, u32[]{:S(2)}) collective-permute-start(f32[480,384]{1,0:T(8,128)S(1)} %collective-permute-done.1.refs_0_), channel_id=1, source_target_pairs={{0,2},{1,3},{2,0},{3,1},{12,14},{13,15},{14,12},{15,13},{16,18},{1... | collective-permute-start | bytes 2211848 | tf_op jit(solution)/shard_map/ppermute | solution.py:333
  56.8 9.1 %collective-permute-start.7 = (f32[480,384]{1,0:T(8,128)S(1)}, f32[480,384]{1,0:T(8,128)S(1)}, u32[]{:S(2)}, u32[]{:S(2)}) collective-permute-start(f32[480,384]{1,0:T(8,128)S(1)} %collective-permute-done.1.refs_0_), channel_id=1, source_target_pairs={{0,1},{1,0},{2,3},{3,2},{12,13},{13,12},{14,15},{15,14},{16,17},{1... | collective-permute-start | bytes 2211848 | tf_op jit(solution)/shard_map/ppermute | solution.py:333
  59.0 8.9 %collective-permute-start.8 = (f32[480,384]{1,0:T(8,128)S(1)}, f32[480,384]{1,0:T(8,128)S(1)}, u32[]{:S(2)}, u32[]{:S(2)}) collective-permute-start(f32[480,384]{1,0:T(8,128)S(1)} %collective-permute-done.2.refs_2_), channel_id=1, source_target_pairs={{0,1},{1,0},{2,3},{3,2},{12,13},{13,12},{14,15},{15,14},{16,17},{1... | collective-permute-start | bytes 2211848 | tf_op jit(solution)/shard_map/ppermute | solution.py:333
  61.4 20.3 %collective-permute-start.9 = (f32[480,384]{1,0:T(8,128)S(1)}, f32[480,384]{1,0:T(8,128)S(1)}, u32[]{:S(2)}, u32[]{:S(2)}) collective-permute-start(f32[480,384]{1,0:T(8,128)S(1)} %collective-permute-done.4.refs_0_), channel_id=1, source_target_pairs={{0,2},{1,3},{2,0},{3,1},{12,14},{13,15},{14,12},{15,13},{16,18},{1... | collective-permute-start | bytes 2211848 | tf_op jit(solution)/shard_map/ppermute | solution.py:333
  63.9 22.2 %collective-permute-start.13 = (f32[480,384]{1,0:T(8,128)}, f32[480,384]{1,0:T(8,128)S(1)}, u32[]{:S(2)}, u32[]{:S(2)}) collective-permute-start(f32[480,384]{1,0:T(8,128)} %collective-permute-done.3), channel_id=1, source_target_pairs={{0,4},{1,5},{2,6},{3,7},{12,8},{13,9},{14,10},{15,11},{16,20},{17,... | collective-permute-start | bytes 2211848 | tf_op jit(solution)/shard_map/ppermute | solution.py:333
  65.2 22.9 %collective-permute-start.16 = (f32[480,384]{1,0:T(8,128)S(1)}, f32[480,384]{1,0:T(8,128)S(1)}, u32[]{:S(2)}, u32[]{:S(2)}) collective-permute-start(f32[480,384]{1,0:T(8,128)S(1)} %fusion.5), channel_id=1, source_target_pairs={{4,6},{5,7},{6,4},{7,5},{8,10},{9,11},{10,8},{11,9},{20,22},{21,23... | collective-permute-start | bytes 2211848 | tf_op jit(solution)/shard_map/ppermute | solution.py:333
  66.0 23.2 %collective-permute-start.12 = (f32[480,384]{1,0:T(8,128)S(1)}, f32[480,384]{1,0:T(8,128)S(1)}, u32[]{:S(2)}, u32[]{:S(2)}) collective-permute-start(f32[480,384]{1,0:T(8,128)S(1)} %fusion.6), channel_id=1, source_target_pairs={{4,6},{5,7},{6,4},{7,5},{8,10},{9,11},{10,8},{11,9},{20,22},{21,23... | collective-permute-start | bytes 2211848 | tf_op jit(solution)/shard_map/ppermute | solution.py:333
  81.7 8.4 %collective-permute-start.10 = (f32[480,384]{1,0:T(8,128)S(1)}, f32[480,384]{1,0:T(8,128)S(1)}, u32[]{:S(2)}, u32[]{:S(2)}) collective-permute-start(f32[480,384]{1,0:T(8,128)S(1)} %collective-permute-done.4.refs_0_), channel_id=1, source_target_pairs={{0,1},{1,0},{2,3},{3,2},{12,13},{13,12},{14,15},{15,14},{16,17},{1... | collective-permute-start | bytes 2211848 | tf_op jit(solution)/shard_map/ppermute | solution.py:333
  89.1 20.3 %collective-permute-start.17 = (f32[480,384]{1,0:T(8,128)}, f32[480,384]{1,0:T(8,128)}, u32[]{:S(2)}, u32[]{:S(2)}) collective-permute-start(f32[480,384]{1,0:T(8,128)} %fusion.2), channel_id=1, source_target_pairs={{4,0},{5,1},{6,2},{7,3},{8,12},{9,13},{10,14},{11,15},{20,16},{21,... | collective-permute-start | bytes 2211848 | tf_op jit(solution)/shard_map/ppermute | solution.py:333
  95.1 8.7 %collective-permute-start.14 = (f32[480,384]{1,0:T(8,128)S(1)}, f32[480,384]{1,0:T(8,128)}, u32[]{:S(2)}, u32[]{:S(2)}) collective-permute-start(f32[480,384]{1,0:T(8,128)S(1)} %broadcast_select_fusion.3.refs_0_), channel_id=1, source_target_pairs={{0,1},{1,0},{2,3},{3,2},{4,5},{5,4},{6,7},{7,6},{8,9},{9,8},{10,11... | collective-permute-start | bytes 2211848 | tf_op jit(solution)/shard_map/ppermute | solution.py:333
  95.2 8.7 %collective-permute-start.15 = (f32[480,384]{1,0:T(8,128)}, f32[480,384]{1,0:T(8,128)}, u32[]{:S(2)}, u32[]{:S(2)}) collective-permute-start(f32[480,384]{1,0:T(8,128)} %broadcast_select_fusion.2.refs_2_), channel_id=1, source_target_pairs={{0,1},{1,0},{2,3},{3,2},{4,5},{5,4},{6,7},{7,6},{8,9},{9,8},{10,11... | collective-permute-start | bytes 2211848 | tf_op jit(solution)/shard_map/ppermute | solution.py:333
  97.7 18.7 %collective-permute-start.18 = (f32[480,384]{1,0:T(8,128)}, f32[480,384]{1,0:T(8,128)}, u32[]{:S(2)}, u32[]{:S(2)}) collective-permute-start(f32[480,384]{1,0:T(8,128)} %broadcast_select_fusion.1.refs_0_), channel_id=1, source_target_pairs={{0,2},{1,3},{2,0},{3,1},{4,6},{5,7},{6,4},{7,5},{8,10},{9,11},{10,... | collective-permute-start | bytes 2211848 | tf_op jit(solution)/shard_map/ppermute | solution.py:333
  117.1 21.3 %collective-permute-start.21 = (f32[480,384]{1,0:T(8,128)S(1)}, f32[480,384]{1,0:T(8,128)S(1)}, u32[]{:S(2)}, u32[]{:S(2)}) collective-permute-start(f32[480,384]{1,0:T(8,128)S(1)} %broadcast_select_fusion), channel_id=1, source_target_pairs={{4,0},{5,1},{6,2},{7,3},{8,12},{9,13},{10,14},{11,15},{20,16},{21,... | collective-permute-start | bytes 2211848 | tf_op jit(solution)/shard_map/ppermute | solution.py:333
  121.7 20.5 %collective-permute-start.26 = (f32[4,96,384]{2,1,0:T(8,128)S(1)}, f32[4,96,384]{2,1,0:T(8,128)S(1)}, u32[]{:S(2)}, u32[]{:S(2)}) collective-permute-start(f32[4,96,384]{2,1,0:T(8,128)S(1)} %get-tuple-element.109), channel_id=1, source_target_pairs={{0,1},{1,0},{2,3},{3,2},{4,5},{5,4},{6,7},{7,6},{8,9},{9,8},{10,11... | collective-permute-start | bytes 1769480 | tf_op jit(solution)/shard_map/ppermute | solution.py:333
  142.9 8.8 %collective-permute-start.28 = (f32[96,384]{1,0:T(8,128)S(1)}, f32[96,384]{1,0:T(8,128)S(1)}, u32[]{:S(2)}, u32[]{:S(2)}) collective-permute-start(f32[96,384]{1,0:T(8,128)S(1)} %get-tuple-element.115), channel_id=1, source_target_pairs={{0,4},{1,5},{2,6},{3,7},{4,0},{5,1},{6,2},{7,3},{8,12},{9,13},{10,... | collective-permute-start | bytes 442376 | tf_op jit(solution)/shard_map/ppermute | solution.py:333
  144.6 8.7 %collective-permute-start.29 = (f32[96,384]{1,0:T(8,128)S(1)}, f32[96,384]{1,0:T(8,128)S(1)}, u32[]{:S(2)}, u32[]{:S(2)}) collective-permute-start(f32[96,384]{1,0:T(8,128)S(1)} %get-tuple-element.116), channel_id=1, source_target_pairs={{0,6},{1,7},{2,4},{3,5},{4,2},{5,3},{6,0},{7,1},{8,14},{9,15},{10,... | collective-permute-start | bytes 442376 | tf_op jit(solution)/shard_map/ppermute | solution.py:333
  145.9 9.4 %collective-permute-start.23 = (f32[96,384]{1,0:T(8,128)S(1)}, f32[96,384]{1,0:T(8,128)S(1)}, u32[]{:S(2)}, u32[]{:S(2)}) collective-permute-start(f32[96,384]{1,0:T(8,128)S(1)} %get-tuple-element.114), channel_id=1, source_target_pairs={{0,2},{1,3},{2,0},{3,1},{4,6},{5,7},{6,4},{7,5},{8,10},{9,11},{10,... | collective-permute-start | bytes 442376 | tf_op jit(solution)/shard_map/ppermute | solution.py:333
  146.5 11.1 %collective-permute-start.24 = (f32[96,384]{1,0:T(8,128)S(1)}, f32[96,384]{1,0:T(8,128)S(1)}, u32[]{:S(2)}, u32[]{:S(2)}) collective-permute-start(f32[96,384]{1,0:T(8,128)S(1)} %get-tuple-element.112), channel_id=1, source_target_pairs={{0,4},{1,5},{2,6},{3,7},{4,0},{5,1},{6,2},{7,3},{8,12},{9,13},{10,... | collective-permute-start | bytes 442376 | tf_op jit(solution)/shard_map/ppermute | solution.py:333
  149.0 10.3 %collective-permute-start.25 = (f32[96,384]{1,0:T(8,128)S(1)}, f32[96,384]{1,0:T(8,128)S(1)}, u32[]{:S(2)}, u32[]{:S(2)}) collective-permute-start(f32[96,384]{1,0:T(8,128)S(1)} %get-tuple-element.113), channel_id=1, source_target_pairs={{0,6},{1,7},{2,4},{3,5},{4,2},{5,3},{6,0},{7,1},{8,14},{9,15},{10,... | collective-permute-start | bytes 442376 | tf_op jit(solution)/shard_map/ppermute | solution.py:333
  (23 other events, 151.8 us)
Sparse Core Ops, SparseCore 0:
  34.5 32.1 all-gather.2

commit v3 on v2

--- a/solution.py
+++ b/solution.py
@@ -426,7 +426,7 @@
         return left[0] + sum(across(left[q], everyone, 2 * q) for q in range(1, half))
 
     crosses = {high: scatter(keep, send)}
-    total, low_parts = after(total, low_parts)
+    total, low_parts, arrived[low] = after(total, low_parts, arrived[low])
     local = apply(one, me, *own_pick, spread(low_parts, everyone))
     so_far, _, keep, send = finish(
         low, chunks, blk, blks, local, arrived[low], pivot, factor, [total], so_far

time: 168 us -> 162 us (0.964)
  waiting for transfers between devices: 35.1 us -> 30.9 us
  Pallas kernels: 56.4 us -> 58.4 us
    ppermute x29, waiting for transfers between devices: 35.1 us -> 30.9 us  [move(): return lax.ppermute(x, ('grp', 'blk'), perm)]
    select_n x1, other arithmetic: 2.08 us -> 0.08 us  [shards(): low_parts = chip_gather(jnp.where(is_same, own[low], sent[low]), everyone)]
    select_n x1, other arithmetic: 0.08 us -> 2.07 us  [shards(): arrived[low] = move(jnp.where(is_same, result, back_sum[low]), backward)]
  transfers between devices with their start and end apart: 31 -> 31, of which waited for: 10 -> 9; matrix products, arithmetic and copies ran while one was open for 9% -> 8% of each run, Pallas kernels for 34% -> 36%
where the time goes in v3:
time: 162 us
  Pallas kernels  58.4 us (36%)
  starting transfers between devices  39.3 us (24%)
  waiting for transfers between devices  30.9 us (19%)
  between operations  14.6 us (9%)
  other arithmetic  10.8 us (7%)
  local copies, waits for them, and re-layouts  6.04 us (4%)
  matrix products  1.62 us (1%)
    ppermute x29, starting transfers between devices, move(): return lax.ppermute(x, ('grp', 'blk'), perm)  39.2 us
    ppermute x29, waiting for transfers between devices, move(): return lax.ppermute(x, ('grp', 'blk'), perm)  30.9 us
    pallas_call x4, Pallas kernels, apply(): pl.pallas_call(apply_kernel, grid_spec=pltpu.PrefetchScalarGridSpec(num_s...  20.1 us
    pallas_call x1, Pallas kernels, second(): pl.pallas_call(functools.partial(second_kernel, steps), grid_spec=pltpu.P...  15.3 us
    pallas_call x1, Pallas kernels, pick(): pl.pallas_call(pick_kernel, grid=(blocks // group,), in_specs=[pl.BlockSp...  11.9 us
    pallas_call x2, Pallas kernels, finish(): pl.pallas_call(functools.partial(finish_kernel, chunk, count), grid=(1,),...  8.97 us
  transfers between devices with their start and end apart: 31, of which 9 were waited for; matrix products, arithmetic and copies ran while one was open for 8% of the time, Pallas kernels for 36%

profile of v3, /device:TPU:0, one launch (start us, length us, event | category | flops | bytes accessed | tf_op | source)
XLA Modules:
  0.0 161.6 jit_solution(781007094905616118)
XLA Ops:
  8.7 3.0 %collective-permute-start.1 = (f32[480,384]{1,0:T(8,128)S(1)}, f32[480,384]{1,0:T(8,128)S(1)}, u32[]{:S(2)}, u32[]{:S(2)}) collective-permute-start(f32[480,384]{1,0:T(8,128)S(1)} %get-tuple-element.88), channel_id=1, source_target_pairs={{0,4},{1,5},{2,6},{3,7},{12,8},{13,9},{14,10},{15,11},{16,20},{17,... | collective-permute-start | bytes 2211848 | tf_op jit(solution)/shard_map/ppermute | solution.py:333
  11.7 3.4 %collective-permute-start.3 = (f32[480,384]{1,0:T(8,128)S(1)}, f32[480,384]{1,0:T(8,128)}, u32[]{:S(2)}, u32[]{:S(2)}) collective-permute-start(f32[480,384]{1,0:T(8,128)S(1)} %get-tuple-element.88), channel_id=1, source_target_pairs={{0,2},{1,3},{2,0},{3,1},{12,14},{13,15},{14,12},{15,13},{16,18},{1... | collective-permute-start | bytes 2211848 | tf_op jit(solution)/shard_map/ppermute | solution.py:333
  19.0 11.9 %pick.1 = (bf16[4,480,480]{2,1,0:T(8,128)(2,1)}, bf16[4,480,480]{2,1,0:T(8,128)(2,1)}) custom-call(s32[480,1]{1,0:T(8,128)} %copy.7.rows_ref, s32[4,1,480]{2,1,0:T(1,128)} %broadcast_subtract_fusion.1.cols_ref, f32[768,3072]{1,0:T(8,128)} %bitcast.54), custom_call_target="tpu_custom_call" | custom-call | bytes 33000000 | tf_op jit(solution)/shard_map/pick/pallas_call | solution.py:103
  31.0 2.4 %collective-permute-start.2 = (f32[480,384]{1,0:T(8,128)S(1)}, f32[480,384]{1,0:T(8,128)}, u32[]{:S(2)}, u32[]{:S(2)}) collective-permute-start(f32[480,384]{1,0:T(8,128)S(1)} %collective-permute-done.1.refs_0_), channel_id=1, source_target_pairs={{0,2},{1,3},{2,0},{3,1},{12,14},{13,15},{14,12},{15,13},{16,18},{1... | collective-permute-start | bytes 2211848 | tf_op jit(solution)/shard_map/ppermute | solution.py:333
  35.9 15.3 %second.1 = (bf16[4,480,480]{2,1,0:T(8,128)(2,1)}, bf16[4,480,480]{2,1,0:T(8,128)(2,1)}, f32[2,480,384]{2,1,0:T(8,128)}, f32[2,480,384]{2,1,0:T(8,128)}, f32[2,480,384]{2,1,0:T(8,128)}, /*index=5*/f32[2,480,384]{2,1,0:T(8,128)}) custom-call(s32[2]{0:T(128)} %pad_add_fusion.1.info, s32[480,1]{1,0:T(8,128)} %copy.8.rows_ref, ...), custom_call_target="tpu_custom_call" | custom-call | bytes 33000000 | tf_op jit(solution)/shard_map/second/pallas_call | solution.py:175
  58.2 2.4 %collective-permute-start.8 = (f32[480,384]{1,0:T(8,128)}, f32[480,384]{1,0:T(8,128)S(1)}, u32[]{:S(2)}, u32[]{:S(2)}) collective-permute-start(f32[480,384]{1,0:T(8,128)} %collective-permute-done.2.refs_2_), channel_id=1, source_target_pairs={{0,1},{1,0},{2,3},{3,2},{12,13},{13,12},{14,15},{15,14},{16,17},{1... | collective-permute-start | bytes 2211848 | tf_op jit(solution)/shard_map/ppermute | solution.py:333
  60.6 2.4 %collective-permute-start.9 = (f32[480,384]{1,0:T(8,128)S(1)}, f32[480,384]{1,0:T(8,128)S(1)}, u32[]{:S(2)}, u32[]{:S(2)}) collective-permute-start(f32[480,384]{1,0:T(8,128)S(1)} %collective-permute-done.4.refs_0_), channel_id=1, source_target_pairs={{0,2},{1,3},{2,0},{3,1},{12,14},{13,15},{14,12},{15,13},{16,18},{1... | collective-permute-start | bytes 2211848 | tf_op jit(solution)/shard_map/ppermute | solution.py:333
  67.8 5.2 %apply.4 = f32[480,384]{1,0:T(8,128)S(1)} custom-call(s32[2]{0:T(128)S(1)} %copy-done.9, bf16[4,480,480]{2,1,0:T(8,128)(2,1)S(1)} %copy-done.5, bf16[4,480,480]{2,1,0:T(8,128)(2,1)S(1)} %copy-done.6, f32[480,384]{1,0:T(8,128)S(1)} %collective-permute-done.1.refs_0_, f32[480,384]{1,0:T(8,128)S(1)} %collective-permute-done.7.refs_1_, ...), custom_call_target="tpu_custom_call" | custom-call | bytes 14850000 | tf_op jit(solution)/shard_map/apply/pallas_call | solution.py:226
  73.0 8.9 %collective-permute-done.9.refs_2_ = f32[480,384]{1,0:T(8,128)S(1)} collective-permute-done((f32[480,384]{1,0:T(8,128)S(1)}, f32[480,384]{1,0:T(8,128)S(1)}, u32[]{:S(2)}, u32[]{:S(2)}) %collective-permute-start.9) | collective-permute-done | bytes 737312 | tf_op jit(solution)/shard_map/ppermute | solution.py:333
  83.8 2.4 %collective-permute-start.11 = (f32[480,384]{1,0:T(8,128)S(1)}, f32[480,384]{1,0:T(8,128)S(1)}, u32[]{:S(2)}, u32[]{:S(2)}) collective-permute-start(f32[480,384]{1,0:T(8,128)S(1)} %collective-permute-done.9.refs_2_), channel_id=1, source_target_pairs={{0,1},{1,0},{2,3},{3,2},{12,13},{13,12},{14,15},{15,14},{16,17},{1... | collective-permute-start | bytes 2211848 | tf_op jit(solution)/shard_map/ppermute | solution.py:333
  90.3 4.1 %apply.5 = f32[480,384]{1,0:T(8,128)S(1)} custom-call(s32[2]{0:T(128)S(1)} %copy-done.9, bf16[4,480,480]{2,1,0:T(8,128)(2,1)S(1)} %copy-done.5, bf16[4,480,480]{2,1,0:T(8,128)(2,1)S(1)} %copy-done.6, f32[480,384]{1,0:T(8,128)S(1)} %collective-permute-done.4.refs_0_, f32[480,384]{1,0:T(8,128)S(1)} %collective-permute-done.10.refs_1_, ...), custom_call_target="tpu_custom_call" | custom-call | bytes 14850000 | tf_op jit(solution)/shard_map/apply/pallas_call | solution.py:226
  97.9 4.7 %collective-permute-start.19 = (f32[480,384]{1,0:T(8,128)}, f32[480,384]{1,0:T(8,128)}, u32[]{:S(2)}, u32[]{:S(2)}) collective-permute-start(f32[480,384]{1,0:T(8,128)} %broadcast_select_fusion), channel_id=1, source_target_pairs={{4,0},{5,1},{6,2},{7,3},{8,12},{9,13},{10,14},{11,15},{20,16},{21,... | collective-permute-start | bytes 2211848 | tf_op jit(solution)/shard_map/ppermute | solution.py:333
  104.3 2.2 %factor.1 = (bf16[768,480]{1,0:T(8,128)(2,1)S(1)}, bf16[768,480]{1,0:T(8,128)(2,1)S(1)}) custom-call(f32[480,768]{1,0:T(8,128)S(1)} %bitcast.53, f32[768,768]{1,0:T(8,128)S(1)} %bitcast.47), custom_call_target="tpu_custom_call" | custom-call | bytes 7260000 | tf_op jit(solution)/shard_map/factor/pallas_call | solution.py:248
  108.2 5.6 %apply.6.refs_0_ = f32[480,384]{1,0:T(8,128)S(1)} custom-call(s32[2]{0:T(128)S(1)} %pad_add_fusion.info, bf16[4,480,480]{2,1,0:T(8,128)(2,1)S(1)} %copy-done.2, bf16[4,480,480]{2,1,0:T(8,128)(2,1)S(1)} %copy-done.3, f32[480,384]{1,0:T(8,128)S(1)} %broadcast_select_fusion.3.refs_0_, f32[480,384]{1,0:T(8,128)} %collective-permute-done.14.refs_1_, ...), custom_call_target="tpu_custom_call" | custom-call | bytes 14850000 | tf_op jit(solution)/shard_map/apply/pallas_call | solution.py:226
  113.8 4.1 %finish.2 = (f32[480,768]{1,0:T(8,128)}, f32[480,384]{1,0:T(8,128)S(1)}, f32[4,96,384]{2,1,0:T(8,128)S(1)}, f32[4,96,384]{2,1,0:T(8,128)S(1)}) custom-call(s32[1]{0:T(128)} %bitcast.info, f32[480,384]{1,0:T(8,128)S(1)} %apply.6.refs_0_, f32[480,384]{1,0:T(8,128)} %collective-permute-done.17.refs_1_, f32[768,768]{1,0:T(8,128)S(1)} %bitcast.49, ...), custom_call_target="tpu_custom_call" | custom-call | bytes 16500000 | tf_op jit(solution)/shard_map/finish/pallas_call | solution.py:293
  117.9 5.9 %collective-permute-done.19.refs_1_ = f32[480,384]{1,0:T(8,128)} collective-permute-done((f32[480,384]{1,0:T(8,128)}, f32[480,384]{1,0:T(8,128)}, u32[]{:S(2)}, u32[]{:S(2)}) %collective-permute-start.19) | collective-permute-done | bytes 737312 | tf_op jit(solution)/shard_map/ppermute | solution.py:333
  124.4 2.7 %collective-permute-done.20.refs_1_ = f32[480,384]{1,0:T(8,128)S(1)} collective-permute-done((f32[480,384]{1,0:T(8,128)S(1)}, f32[480,384]{1,0:T(8,128)S(1)}, u32[]{:S(2)}, u32[]{:S(2)}) %collective-permute-start.20) | collective-permute-done | bytes 737312 | tf_op jit(solution)/shard_map/ppermute | solution.py:333
  127.8 5.2 %apply.7.refs_0_ = f32[480,384]{1,0:T(8,128)S(1)} custom-call(s32[2]{0:T(128)S(1)} %pad_add_fusion.info, bf16[4,480,480]{2,1,0:T(8,128)(2,1)S(1)} %copy-done.2, bf16[4,480,480]{2,1,0:T(8,128)(2,1)S(1)} %copy-done.3, f32[480,384]{1,0:T(8,128)S(1)} %broadcast_select_fusion.1.refs_0_, f32[480,384]{1,0:T(8,128)S(1)} %collective-permute-done.20.refs_1_, ...), custom_call_target="tpu_custom_call" | custom-call | bytes 14850000 | tf_op jit(solution)/shard_map/apply/pallas_call | solution.py:226
  133.0 4.9 %finish.3 = (f32[480,768]{1,0:T(8,128)}, f32[480,384]{1,0:T(8,128)}, f32[4,96,384]{2,1,0:T(8,128)S(1)}, f32[4,96,384]{2,1,0:T(8,128)S(1)}) custom-call(s32[1]{0:T(128)} %bitcast.info, f32[480,384]{1,0:T(8,128)S(1)} %apply.7.refs_0_, f32[480,384]{1,0:T(8,128)} %collective-permute-done.19.refs_1_, ...), custom_call_target="tpu_custom_call", output_to_operand_aliasing={{0}: (7, {})} | custom-call | bytes 16500000 | tf_op jit(solution)/shard_map/finish/pallas_call | solution.py:293
  139.3 2.6 %collective-permute-start.29 = (f32[96,384]{1,0:T(8,128)S(1)}, f32[96,384]{1,0:T(8,128)S(1)}, u32[]{:S(2)}, u32[]{:S(2)}) collective-permute-start(f32[96,384]{1,0:T(8,128)S(1)} %get-tuple-element.118), channel_id=1, source_target_pairs={{0,6},{1,7},{2,4},{3,5},{4,2},{5,3},{6,0},{7,1},{8,14},{9,15},{10,... | collective-permute-start | bytes 442376 | tf_op jit(solution)/shard_map/ppermute | solution.py:333
  143.0 2.1 %collective-permute-done.27 = f32[96,384]{1,0:T(8,128)S(1)} collective-permute-done((f32[96,384]{1,0:T(8,128)S(1)}, f32[96,384]{1,0:T(8,128)S(1)}, u32[]{:S(2)}, u32[]{:S(2)}) %collective-permute-start.27) | collective-permute-done | bytes 147488 | tf_op jit(solution)/shard_map/ppermute | solution.py:333
  145.6 2.9 %collective-permute-done.28 = f32[96,384]{1,0:T(8,128)S(1)} collective-permute-done((f32[96,384]{1,0:T(8,128)S(1)}, f32[96,384]{1,0:T(8,128)S(1)}, u32[]{:S(2)}, u32[]{:S(2)}) %collective-permute-start.28) | collective-permute-done | bytes 147488 | tf_op jit(solution)/shard_map/ppermute | solution.py:333
  148.5 2.9 %collective-permute-done.23 = f32[96,384]{1,0:T(8,128)S(1)} collective-permute-done((f32[96,384]{1,0:T(8,128)S(1)}, f32[96,384]{1,0:T(8,128)S(1)}, u32[]{:S(2)}, u32[]{:S(2)}) %collective-permute-start.23) | collective-permute-done | bytes 147488 | tf_op jit(solution)/shard_map/ppermute | solution.py:333
  151.5 2.5 %collective-permute-done.24 = f32[96,384]{1,0:T(8,128)S(1)} collective-permute-done((f32[96,384]{1,0:T(8,128)S(1)}, f32[96,384]{1,0:T(8,128)S(1)}, u32[]{:S(2)}, u32[]{:S(2)}) %collective-permute-start.24) | collective-permute-done | bytes 147488 | tf_op jit(solution)/shard_map/ppermute | solution.py:333
  (109 shorter events, 37.2 us)
Async XLA Ops:
  7.2 88.1 %all-gather.3.cloned.1.call-start = ((), (), s32[]{:S(2)}) async-start(), calls=%async_computation | async-start | bytes 2654208 | tf_op jit(solution)/shard_map/all_gather | solution.py:361
  8.7 22.3 %collective-permute-start.1 = (f32[480,384]{1,0:T(8,128)S(1)}, f32[480,384]{1,0:T(8,128)S(1)}, u32[]{:S(2)}, u32[]{:S(2)}) collective-permute-start(f32[480,384]{1,0:T(8,128)S(1)} %get-tuple-element.88), channel_id=1, source_target_pairs={{0,4},{1,5},{2,6},{3,7},{12,8},{13,9},{14,10},{15,11},{16,20},{17,... | collective-permute-start | bytes 2211848 | tf_op jit(solution)/shard_map/ppermute | solution.py:333
  11.7 39.5 %collective-permute-start.3 = (f32[480,384]{1,0:T(8,128)S(1)}, f32[480,384]{1,0:T(8,128)}, u32[]{:S(2)}, u32[]{:S(2)}) collective-permute-start(f32[480,384]{1,0:T(8,128)S(1)} %get-tuple-element.88), channel_id=1, source_target_pairs={{0,2},{1,3},{2,0},{3,1},{12,14},{13,15},{14,12},{15,13},{16,18},{1... | collective-permute-start | bytes 2211848 | tf_op jit(solution)/shard_map/ppermute | solution.py:333
  15.1 15.8 %collective-permute-start = (s32[3840]{0:T(1024)S(1)}, s32[3840]{0:T(1024)S(1)}, u32[]{:S(2)}, u32[]{:S(2)}) collective-permute-start(s32[3840]{0:T(1024)S(1)} %reduce), channel_id=1, source_target_pairs={{0,8},{8,0},{16,24},{24,16},{1,9},{9,1},{17,25},{25,17},{2,10},{10... | collective-permute-start | bytes 46088 | tf_op jit(solution)/shard_map/ppermute | solution.py:360
  15.2 36.0 %collective-permute-start.4 = (f32[480,384]{1,0:T(8,128)S(1)}, f32[480,384]{1,0:T(8,128)S(1)}, u32[]{:S(2)}, u32[]{:S(2)}) collective-permute-start(f32[480,384]{1,0:T(8,128)S(1)} %get-tuple-element.70), channel_id=1, source_target_pairs={{0,4},{1,5},{2,6},{3,7},{12,8},{13,9},{14,10},{15,11},{16,20},{17,... | collective-permute-start | bytes 2211848 | tf_op jit(solution)/shard_map/ppermute | solution.py:333
  31.0 22.3 %collective-permute-start.2 = (f32[480,384]{1,0:T(8,128)S(1)}, f32[480,384]{1,0:T(8,128)}, u32[]{:S(2)}, u32[]{:S(2)}) collective-permute-start(f32[480,384]{1,0:T(8,128)S(1)} %collective-permute-done.1.refs_0_), channel_id=1, source_target_pairs={{0,2},{1,3},{2,0},{3,1},{12,14},{13,15},{14,12},{15,13},{16,18},{1... | collective-permute-start | bytes 2211848 | tf_op jit(solution)/shard_map/ppermute | solution.py:333
  56.1 9.1 %collective-permute-start.7 = (f32[480,384]{1,0:T(8,128)S(1)}, f32[480,384]{1,0:T(8,128)S(1)}, u32[]{:S(2)}, u32[]{:S(2)}) collective-permute-start(f32[480,384]{1,0:T(8,128)S(1)} %collective-permute-done.1.refs_0_), channel_id=1, source_target_pairs={{0,1},{1,0},{2,3},{3,2},{12,13},{13,12},{14,15},{15,14},{16,17},{1... | collective-permute-start | bytes 2211848 | tf_op jit(solution)/shard_map/ppermute | solution.py:333
  58.2 8.0 %collective-permute-start.8 = (f32[480,384]{1,0:T(8,128)}, f32[480,384]{1,0:T(8,128)S(1)}, u32[]{:S(2)}, u32[]{:S(2)}) collective-permute-start(f32[480,384]{1,0:T(8,128)} %collective-permute-done.2.refs_2_), channel_id=1, source_target_pairs={{0,1},{1,0},{2,3},{3,2},{12,13},{13,12},{14,15},{15,14},{16,17},{1... | collective-permute-start | bytes 2211848 | tf_op jit(solution)/shard_map/ppermute | solution.py:333
  60.6 21.2 %collective-permute-start.9 = (f32[480,384]{1,0:T(8,128)S(1)}, f32[480,384]{1,0:T(8,128)S(1)}, u32[]{:S(2)}, u32[]{:S(2)}) collective-permute-start(f32[480,384]{1,0:T(8,128)S(1)} %collective-permute-done.4.refs_0_), channel_id=1, source_target_pairs={{0,2},{1,3},{2,0},{3,1},{12,14},{13,15},{14,12},{15,13},{16,18},{1... | collective-permute-start | bytes 2211848 | tf_op jit(solution)/shard_map/ppermute | solution.py:333
  63.0 20.7 %collective-permute-start.13 = (f32[480,384]{1,0:T(8,128)}, f32[480,384]{1,0:T(8,128)S(1)}, u32[]{:S(2)}, u32[]{:S(2)}) collective-permute-start(f32[480,384]{1,0:T(8,128)} %collective-permute-done.3), channel_id=1, source_target_pairs={{0,4},{1,5},{2,6},{3,7},{12,8},{13,9},{14,10},{15,11},{16,20},{17,... | collective-permute-start | bytes 2211848 | tf_op jit(solution)/shard_map/ppermute | solution.py:333
  64.4 23.9 %collective-permute-start.16 = (f32[480,384]{1,0:T(8,128)S(1)}, f32[480,384]{1,0:T(8,128)S(1)}, u32[]{:S(2)}, u32[]{:S(2)}) collective-permute-start(f32[480,384]{1,0:T(8,128)S(1)} %fusion.5), channel_id=1, source_target_pairs={{4,6},{5,7},{6,4},{7,5},{8,10},{9,11},{10,8},{11,9},{20,22},{21,23... | collective-permute-start | bytes 2211848 | tf_op jit(solution)/shard_map/ppermute | solution.py:333
  65.2 24.1 %collective-permute-start.12 = (f32[480,384]{1,0:T(8,128)S(1)}, f32[480,384]{1,0:T(8,128)S(1)}, u32[]{:S(2)}, u32[]{:S(2)}) collective-permute-start(f32[480,384]{1,0:T(8,128)S(1)} %fusion.6), channel_id=1, source_target_pairs={{4,6},{5,7},{6,4},{7,5},{8,10},{9,11},{10,8},{11,9},{20,22},{21,23... | collective-permute-start | bytes 2211848 | tf_op jit(solution)/shard_map/ppermute | solution.py:333
  66.2 51.7 %collective-permute-start.18 = (f32[480,384]{1,0:T(8,128)S(1)}, f32[480,384]{1,0:T(8,128)}, u32[]{:S(2)}, u32[]{:S(2)}) collective-permute-start(f32[480,384]{1,0:T(8,128)S(1)} %broadcast_select_fusion.1.refs_0_), channel_id=1, source_target_pairs={{0,2},{1,3},{2,0},{3,1},{4,6},{5,7},{6,4},{7,5},{8,10},{9,11},{10,... | collective-permute-start | bytes 2211848 | tf_op jit(solution)/shard_map/ppermute | solution.py:333
  81.9 8.5 %collective-permute-start.10 = (f32[480,384]{1,0:T(8,128)S(1)}, f32[480,384]{1,0:T(8,128)S(1)}, u32[]{:S(2)}, u32[]{:S(2)}) collective-permute-start(f32[480,384]{1,0:T(8,128)S(1)} %collective-permute-done.4.refs_0_), channel_id=1, source_target_pairs={{0,1},{1,0},{2,3},{3,2},{12,13},{13,12},{14,15},{15,14},{16,17},{1... | collective-permute-start | bytes 2211848 | tf_op jit(solution)/shard_map/ppermute | solution.py:333
  89.3 24.5 %collective-permute-start.17 = (f32[480,384]{1,0:T(8,128)}, f32[480,384]{1,0:T(8,128)}, u32[]{:S(2)}, u32[]{:S(2)}) collective-permute-start(f32[480,384]{1,0:T(8,128)} %fusion.2), channel_id=1, source_target_pairs={{4,0},{5,1},{6,2},{7,3},{8,12},{9,13},{10,14},{11,15},{20,16},{21,... | collective-permute-start | bytes 2211848 | tf_op jit(solution)/shard_map/ppermute | solution.py:333
  95.3 12.8 %collective-permute-start.14 = (f32[480,384]{1,0:T(8,128)S(1)}, f32[480,384]{1,0:T(8,128)}, u32[]{:S(2)}, u32[]{:S(2)}) collective-permute-start(f32[480,384]{1,0:T(8,128)S(1)} %broadcast_select_fusion.3.refs_0_), channel_id=1, source_target_pairs={{0,1},{1,0},{2,3},{3,2},{4,5},{5,4},{6,7},{7,6},{8,9},{9,8},{10,11... | collective-permute-start | bytes 2211848 | tf_op jit(solution)/shard_map/ppermute | solution.py:333
  95.3 12.8 %collective-permute-start.15 = (f32[480,384]{1,0:T(8,128)}, f32[480,384]{1,0:T(8,128)}, u32[]{:S(2)}, u32[]{:S(2)}) collective-permute-start(f32[480,384]{1,0:T(8,128)} %broadcast_select_fusion.2.refs_2_), channel_id=1, source_target_pairs={{0,1},{1,0},{2,3},{3,2},{4,5},{5,4},{6,7},{7,6},{8,9},{9,8},{10,11... | collective-permute-start | bytes 2211848 | tf_op jit(solution)/shard_map/ppermute | solution.py:333
  97.9 26.0 %collective-permute-start.19 = (f32[480,384]{1,0:T(8,128)}, f32[480,384]{1,0:T(8,128)}, u32[]{:S(2)}, u32[]{:S(2)}) collective-permute-start(f32[480,384]{1,0:T(8,128)} %broadcast_select_fusion), channel_id=1, source_target_pairs={{4,0},{5,1},{6,2},{7,3},{8,12},{9,13},{10,14},{11,15},{20,16},{21,... | collective-permute-start | bytes 2211848 | tf_op jit(solution)/shard_map/ppermute | solution.py:333
  124.4 13.9 %collective-permute-start.26 = (f32[4,96,384]{2,1,0:T(8,128)S(1)}, f32[4,96,384]{2,1,0:T(8,128)S(1)}, u32[]{:S(2)}, u32[]{:S(2)}) collective-permute-start(f32[4,96,384]{2,1,0:T(8,128)S(1)} %get-tuple-element.111), channel_id=1, source_target_pairs={{0,1},{1,0},{2,3},{3,2},{4,5},{5,4},{6,7},{7,6},{8,9},{9,8},{10,11... | collective-permute-start | bytes 1769480 | tf_op jit(solution)/shard_map/ppermute | solution.py:333
  138.9 9.6 %collective-permute-start.28 = (f32[96,384]{1,0:T(8,128)S(1)}, f32[96,384]{1,0:T(8,128)S(1)}, u32[]{:S(2)}, u32[]{:S(2)}) collective-permute-start(f32[96,384]{1,0:T(8,128)S(1)} %get-tuple-element.117), channel_id=1, source_target_pairs={{0,4},{1,5},{2,6},{3,7},{4,0},{5,1},{6,2},{7,3},{8,12},{9,13},{10,... | collective-permute-start | bytes 442376 | tf_op jit(solution)/shard_map/ppermute | solution.py:333
  139.3 9.2 %collective-permute-start.29 = (f32[96,384]{1,0:T(8,128)S(1)}, f32[96,384]{1,0:T(8,128)S(1)}, u32[]{:S(2)}, u32[]{:S(2)}) collective-permute-start(f32[96,384]{1,0:T(8,128)S(1)} %get-tuple-element.118), channel_id=1, source_target_pairs={{0,6},{1,7},{2,4},{3,5},{4,2},{5,3},{6,0},{7,1},{8,14},{9,15},{10,... | collective-permute-start | bytes 442376 | tf_op jit(solution)/shard_map/ppermute | solution.py:333
  142.0 9.5 %collective-permute-start.23 = (f32[96,384]{1,0:T(8,128)S(1)}, f32[96,384]{1,0:T(8,128)S(1)}, u32[]{:S(2)}, u32[]{:S(2)}) collective-permute-start(f32[96,384]{1,0:T(8,128)S(1)} %get-tuple-element.116), channel_id=1, source_target_pairs={{0,2},{1,3},{2,0},{3,1},{4,6},{5,7},{6,4},{7,5},{8,10},{9,11},{10,... | collective-permute-start | bytes 442376 | tf_op jit(solution)/shard_map/ppermute | solution.py:333
  142.6 11.4 %collective-permute-start.24 = (f32[96,384]{1,0:T(8,128)S(1)}, f32[96,384]{1,0:T(8,128)S(1)}, u32[]{:S(2)}, u32[]{:S(2)}) collective-permute-start(f32[96,384]{1,0:T(8,128)S(1)} %get-tuple-element.114), channel_id=1, source_target_pairs={{0,4},{1,5},{2,6},{3,7},{4,0},{5,1},{6,2},{7,3},{8,12},{9,13},{10,... | collective-permute-start | bytes 442376 | tf_op jit(solution)/shard_map/ppermute | solution.py:333
  145.1 8.9 %collective-permute-start.25 = (f32[96,384]{1,0:T(8,128)S(1)}, f32[96,384]{1,0:T(8,128)S(1)}, u32[]{:S(2)}, u32[]{:S(2)}) collective-permute-start(f32[96,384]{1,0:T(8,128)S(1)} %get-tuple-element.115), channel_id=1, source_target_pairs={{0,6},{1,7},{2,4},{3,5},{4,2},{5,3},{6,0},{7,1},{8,14},{9,15},{10,... | collective-permute-start | bytes 442376 | tf_op jit(solution)/shard_map/ppermute | solution.py:333
  (22 other events, 121.1 us)
Sparse Core Ops, SparseCore 0:
  33.6 32.1 all-gather.2

commit v4 on v3

--- a/solution.py
+++ b/solution.py
@@ -72,10 +72,29 @@
     hot_ref[...] = (at_row == rows_ref[...]).astype(F32).astype(BF16)
 
 
+def pick_rows(hot, piece):
+    picked, height = hot.shape
+    slack, deep = height - picked, 256
+    if height != 3 * deep or slack > 2 * deep or picked % 16 or slack % 32:
+        return dot1(hot, piece)
+    until, since = deep, 2 * deep - slack
+    first = dot1(hot[:until, :deep], piece[:deep])
+    middle = dot1(hot[:, deep : 2 * deep], piece[deep : 2 * deep])
+    last = dot1(hot[since:, 2 * deep :], piece[2 * deep :])
+    return jnp.concatenate(
+        [
+            first[:since] + middle[:since],
+            first[since:] + middle[since:until] + last[: until - since],
+            middle[until:] + last[until - since :],
+        ],
+        axis=0,
+    )
+
+
 def pick_block(block, cols_ref, hot_ref, high_ref, low_ref):
     picked = hot_ref.shape[0]
     pair = split(block)
-    both = jnp.concatenate([dot1(hot_ref[...], piece) for piece in pair], axis=0).astype(BF16)
+    both = jnp.concatenate([pick_rows(hot_ref[...], piece) for piece in pair], axis=0).astype(BF16)
     at_col = lax.broadcasted_iota(jnp.int32, (block.shape[1], picked), 0)
     for q in range(cols_ref.shape[0]):
         col_hot = (at_col == cols_ref[q]).astype(F32).astype(BF16)
@@ -413,7 +432,7 @@
 
     height = order // blks
     gram_cols = lax.dynamic_slice_in_dim(pivot, blk * height, height, 1)
-    gram = jnp.einsum("ar,ac->rc", gram_cols, pivot, precision=lax.Precision.HIGHEST)
+    gram = jnp.einsum("ar,ac->rc", gram_cols, pivot, precision=lax.Precision.HIGH)
     factor = factor_of(lower, pivot)
     local = apply(one, me, *own_pick, spread(high_parts, everyone))
     factor, gram, local = after(factor, gram, local)

time: 162 us -> 162 us (level)
  no operation moved by 1% of the time
where the time goes in v4:
time: 162 us; the launch traced here: 161 us
  Pallas kernels  57.7 us (36%)
  starting transfers between devices  39.6 us (24%)
  waiting for transfers between devices  31.2 us (19%)
  between operations  14.6 us (9%)
  other arithmetic  10.8 us (7%)
  local copies, waits for them, and re-layouts  6.56 us (4%)
    ppermute x29, starting transfers between devices, move(): return lax.ppermute(x, ('grp', 'blk'), perm)  39.5 us
    ppermute x29, waiting for transfers between devices, move(): return lax.ppermute(x, ('grp', 'blk'), perm)  31.2 us
    pallas_call x4, Pallas kernels, apply(): pl.pallas_call(apply_kernel, grid_spec=pltpu.PrefetchScalarGridSpec(num_s...  20 us
    pallas_call x1, Pallas kernels, second(): pl.pallas_call(functools.partial(second_kernel, steps), grid_spec=pltpu.P...  14.8 us
    pallas_call x1, Pallas kernels, pick(): pl.pallas_call(pick_kernel, grid=(blocks // group,), in_specs=[pl.BlockSp...  11.7 us
    pallas_call x2, Pallas kernels, finish(): pl.pallas_call(functools.partial(finish_kernel, chunk, count), grid=(1,),...  8.97 us
  transfers between devices with their start and end apart: 31, of which 9 were waited for; matrix products, arithmetic and copies ran while one was open for 8% of the time, Pallas kernels for 36%

profile of v4, /device:TPU:0, one launch (start us, length us, event | category | flops | bytes accessed | tf_op | source)
XLA Modules:
  0.0 161.5 jit_solution(5455120569343826599)
XLA Ops:
  8.7 3.0 %collective-permute-start.1 = (f32[480,384]{1,0:T(8,128)S(1)}, f32[480,384]{1,0:T(8,128)S(1)}, u32[]{:S(2)}, u32[]{:S(2)}) collective-permute-start(f32[480,384]{1,0:T(8,128)S(1)} %get-tuple-element.88), channel_id=1, source_target_pairs={{0,4},{1,5},{2,6},{3,7},{12,8},{13,9},{14,10},{15,11},{16,20},{17,... | collective-permute-start | bytes 2211848 | tf_op jit(solution)/shard_map/ppermute | solution.py:352
  11.7 3.4 %collective-permute-start.3 = (f32[480,384]{1,0:T(8,128)S(1)}, f32[480,384]{1,0:T(8,128)}, u32[]{:S(2)}, u32[]{:S(2)}) collective-permute-start(f32[480,384]{1,0:T(8,128)S(1)} %get-tuple-element.88), channel_id=1, source_target_pairs={{0,2},{1,3},{2,0},{3,1},{12,14},{13,15},{14,12},{15,13},{16,18},{1... | collective-permute-start | bytes 2211848 | tf_op jit(solution)/shard_map/ppermute | solution.py:352
  19.0 11.7 %pick.1 = (bf16[4,480,480]{2,1,0:T(8,128)(2,1)}, bf16[4,480,480]{2,1,0:T(8,128)(2,1)}) custom-call(s32[480,1]{1,0:T(8,128)} %copy.7.rows_ref, s32[4,1,480]{2,1,0:T(1,128)} %broadcast_subtract_fusion.1.cols_ref, f32[768,3072]{1,0:T(8,128)} %bitcast.54), custom_call_target="tpu_custom_call" | custom-call | bytes 33000000 | tf_op jit(solution)/shard_map/pick/pallas_call | solution.py:122
  30.8 2.5 %collective-permute-start.2 = (f32[480,384]{1,0:T(8,128)S(1)}, f32[480,384]{1,0:T(8,128)}, u32[]{:S(2)}, u32[]{:S(2)}) collective-permute-start(f32[480,384]{1,0:T(8,128)S(1)} %collective-permute-done.1.refs_0_), channel_id=1, source_target_pairs={{0,2},{1,3},{2,0},{3,1},{12,14},{13,15},{14,12},{15,13},{16,18},{1... | collective-permute-start | bytes 2211848 | tf_op jit(solution)/shard_map/ppermute | solution.py:352
  35.8 14.8 %second.1 = (bf16[4,480,480]{2,1,0:T(8,128)(2,1)}, bf16[4,480,480]{2,1,0:T(8,128)(2,1)}, f32[2,480,384]{2,1,0:T(8,128)}, f32[2,480,384]{2,1,0:T(8,128)}, f32[2,480,384]{2,1,0:T(8,128)}, /*index=5*/f32[2,480,384]{2,1,0:T(8,128)}) custom-call(s32[2]{0:T(128)} %pad_add_fusion.1.info, s32[480,1]{1,0:T(8,128)} %copy.8.rows_ref, ...), custom_call_target="tpu_custom_call" | custom-call | bytes 33000000 | tf_op jit(solution)/shard_map/second/pallas_call | solution.py:194
  50.7 2.4 %collective-permute-done.2.refs_2_ = f32[480,384]{1,0:T(8,128)} collective-permute-done((f32[480,384]{1,0:T(8,128)S(1)}, f32[480,384]{1,0:T(8,128)}, u32[]{:S(2)}, u32[]{:S(2)}) %collective-permute-start.2) | collective-permute-done | bytes 737312 | tf_op jit(solution)/shard_map/ppermute | solution.py:352
  58.0 2.4 %collective-permute-start.8 = (f32[480,384]{1,0:T(8,128)}, f32[480,384]{1,0:T(8,128)S(1)}, u32[]{:S(2)}, u32[]{:S(2)}) collective-permute-start(f32[480,384]{1,0:T(8,128)} %collective-permute-done.2.refs_2_), channel_id=1, source_target_pairs={{0,1},{1,0},{2,3},{3,2},{12,13},{13,12},{14,15},{15,14},{16,17},{1... | collective-permute-start | bytes 2211848 | tf_op jit(solution)/shard_map/ppermute | solution.py:352
  60.4 2.4 %collective-permute-start.9 = (f32[480,384]{1,0:T(8,128)S(1)}, f32[480,384]{1,0:T(8,128)S(1)}, u32[]{:S(2)}, u32[]{:S(2)}) collective-permute-start(f32[480,384]{1,0:T(8,128)S(1)} %collective-permute-done.4.refs_0_), channel_id=1, source_target_pairs={{0,2},{1,3},{2,0},{3,1},{12,14},{13,15},{14,12},{15,13},{16,18},{1... | collective-permute-start | bytes 2211848 | tf_op jit(solution)/shard_map/ppermute | solution.py:352
  67.6 5.2 %apply.4 = f32[480,384]{1,0:T(8,128)S(1)} custom-call(s32[2]{0:T(128)S(1)} %copy-done.9, bf16[4,480,480]{2,1,0:T(8,128)(2,1)S(1)} %copy-done.5, bf16[4,480,480]{2,1,0:T(8,128)(2,1)S(1)} %copy-done.6, f32[480,384]{1,0:T(8,128)S(1)} %collective-permute-done.1.refs_0_, f32[480,384]{1,0:T(8,128)S(1)} %collective-permute-done.7.refs_1_, ...), custom_call_target="tpu_custom_call" | custom-call | bytes 14850000 | tf_op jit(solution)/shard_map/apply/pallas_call | solution.py:245
  72.8 8.9 %collective-permute-done.9.refs_2_ = f32[480,384]{1,0:T(8,128)S(1)} collective-permute-done((f32[480,384]{1,0:T(8,128)S(1)}, f32[480,384]{1,0:T(8,128)S(1)}, u32[]{:S(2)}, u32[]{:S(2)}) %collective-permute-start.9) | collective-permute-done | bytes 737312 | tf_op jit(solution)/shard_map/ppermute | solution.py:352
  83.6 2.4 %collective-permute-start.11 = (f32[480,384]{1,0:T(8,128)S(1)}, f32[480,384]{1,0:T(8,128)S(1)}, u32[]{:S(2)}, u32[]{:S(2)}) collective-permute-start(f32[480,384]{1,0:T(8,128)S(1)} %collective-permute-done.9.refs_2_), channel_id=1, source_target_pairs={{0,1},{1,0},{2,3},{3,2},{12,13},{13,12},{14,15},{15,14},{16,17},{1... | collective-permute-start | bytes 2211848 | tf_op jit(solution)/shard_map/ppermute | solution.py:352
  90.1 4.1 %apply.5 = f32[480,384]{1,0:T(8,128)S(1)} custom-call(s32[2]{0:T(128)S(1)} %copy-done.9, bf16[4,480,480]{2,1,0:T(8,128)(2,1)S(1)} %copy-done.5, bf16[4,480,480]{2,1,0:T(8,128)(2,1)S(1)} %copy-done.6, f32[480,384]{1,0:T(8,128)S(1)} %collective-permute-done.4.refs_0_, f32[480,384]{1,0:T(8,128)S(1)} %collective-permute-done.10.refs_1_, ...), custom_call_target="tpu_custom_call" | custom-call | bytes 14850000 | tf_op jit(solution)/shard_map/apply/pallas_call | solution.py:245
  97.7 4.7 %collective-permute-start.19 = (f32[480,384]{1,0:T(8,128)}, f32[480,384]{1,0:T(8,128)}, u32[]{:S(2)}, u32[]{:S(2)}) collective-permute-start(f32[480,384]{1,0:T(8,128)} %broadcast_select_fusion), channel_id=1, source_target_pairs={{4,0},{5,1},{6,2},{7,3},{8,12},{9,13},{10,14},{11,15},{20,16},{21,... | collective-permute-start | bytes 2211848 | tf_op jit(solution)/shard_map/ppermute | solution.py:352
  104.1 2.2 %factor.1 = (bf16[768,480]{1,0:T(8,128)(2,1)S(1)}, bf16[768,480]{1,0:T(8,128)(2,1)S(1)}) custom-call(f32[480,768]{1,0:T(8,128)S(1)} %bitcast.53, f32[768,768]{1,0:T(8,128)S(1)} %bitcast.47), custom_call_target="tpu_custom_call" | custom-call | bytes 7260000 | tf_op jit(solution)/shard_map/factor/pallas_call | solution.py:267
  107.8 5.5 %apply.6.refs_0_ = f32[480,384]{1,0:T(8,128)S(1)} custom-call(s32[2]{0:T(128)S(1)} %pad_add_fusion.info, bf16[4,480,480]{2,1,0:T(8,128)(2,1)S(1)} %copy-done.2, bf16[4,480,480]{2,1,0:T(8,128)(2,1)S(1)} %copy-done.3, f32[480,384]{1,0:T(8,128)S(1)} %broadcast_select_fusion.3.refs_0_, f32[480,384]{1,0:T(8,128)} %collective-permute-done.14.refs_1_, ...), custom_call_target="tpu_custom_call" | custom-call | bytes 14850000 | tf_op jit(solution)/shard_map/apply/pallas_call | solution.py:245
  113.4 4.1 %finish.2 = (f32[480,768]{1,0:T(8,128)}, f32[480,384]{1,0:T(8,128)S(1)}, f32[4,96,384]{2,1,0:T(8,128)S(1)}, f32[4,96,384]{2,1,0:T(8,128)S(1)}) custom-call(s32[1]{0:T(128)} %bitcast.info, f32[480,384]{1,0:T(8,128)S(1)} %apply.6.refs_0_, f32[480,384]{1,0:T(8,128)} %collective-permute-done.17.refs_1_, f32[768,768]{1,0:T(8,128)S(1)} %bitcast.49, ...), custom_call_target="tpu_custom_call" | custom-call | bytes 16500000 | tf_op jit(solution)/shard_map/finish/pallas_call | solution.py:312
  117.5 6.2 %collective-permute-done.19.refs_1_ = f32[480,384]{1,0:T(8,128)} collective-permute-done((f32[480,384]{1,0:T(8,128)}, f32[480,384]{1,0:T(8,128)}, u32[]{:S(2)}, u32[]{:S(2)}) %collective-permute-start.19) | collective-permute-done | bytes 737312 | tf_op jit(solution)/shard_map/ppermute | solution.py:352
  124.2 2.7 %collective-permute-done.20.refs_1_ = f32[480,384]{1,0:T(8,128)S(1)} collective-permute-done((f32[480,384]{1,0:T(8,128)S(1)}, f32[480,384]{1,0:T(8,128)S(1)}, u32[]{:S(2)}, u32[]{:S(2)}) %collective-permute-start.20) | collective-permute-done | bytes 737312 | tf_op jit(solution)/shard_map/ppermute | solution.py:352
  127.6 5.2 %apply.7.refs_0_ = f32[480,384]{1,0:T(8,128)S(1)} custom-call(s32[2]{0:T(128)S(1)} %pad_add_fusion.info, bf16[4,480,480]{2,1,0:T(8,128)(2,1)S(1)} %copy-done.2, bf16[4,480,480]{2,1,0:T(8,128)(2,1)S(1)} %copy-done.3, f32[480,384]{1,0:T(8,128)S(1)} %broadcast_select_fusion.1.refs_0_, f32[480,384]{1,0:T(8,128)S(1)} %collective-permute-done.20.refs_1_, ...), custom_call_target="tpu_custom_call" | custom-call | bytes 14850000 | tf_op jit(solution)/shard_map/apply/pallas_call | solution.py:245
  132.8 4.9 %finish.3 = (f32[480,768]{1,0:T(8,128)}, f32[480,384]{1,0:T(8,128)}, f32[4,96,384]{2,1,0:T(8,128)S(1)}, f32[4,96,384]{2,1,0:T(8,128)S(1)}) custom-call(s32[1]{0:T(128)} %bitcast.info, f32[480,384]{1,0:T(8,128)S(1)} %apply.7.refs_0_, f32[480,384]{1,0:T(8,128)} %collective-permute-done.19.refs_1_, ...), custom_call_target="tpu_custom_call", output_to_operand_aliasing={{0}: (7, {})} | custom-call | bytes 16500000 | tf_op jit(solution)/shard_map/finish/pallas_call | solution.py:312
  139.3 2.4 %collective-permute-start.29 = (f32[96,384]{1,0:T(8,128)S(1)}, f32[96,384]{1,0:T(8,128)S(1)}, u32[]{:S(2)}, u32[]{:S(2)}) collective-permute-start(f32[96,384]{1,0:T(8,128)S(1)} %get-tuple-element.118), channel_id=1, source_target_pairs={{0,6},{1,7},{2,4},{3,5},{4,2},{5,3},{6,0},{7,1},{8,14},{9,15},{10,... | collective-permute-start | bytes 442376 | tf_op jit(solution)/shard_map/ppermute | solution.py:352
  145.5 2.9 %collective-permute-done.28 = f32[96,384]{1,0:T(8,128)S(1)} collective-permute-done((f32[96,384]{1,0:T(8,128)S(1)}, f32[96,384]{1,0:T(8,128)S(1)}, u32[]{:S(2)}, u32[]{:S(2)}) %collective-permute-start.28) | collective-permute-done | bytes 147488 | tf_op jit(solution)/shard_map/ppermute | solution.py:352
  148.4 2.9 %collective-permute-done.23 = f32[96,384]{1,0:T(8,128)S(1)} collective-permute-done((f32[96,384]{1,0:T(8,128)S(1)}, f32[96,384]{1,0:T(8,128)S(1)}, u32[]{:S(2)}, u32[]{:S(2)}) %collective-permute-start.23) | collective-permute-done | bytes 147488 | tf_op jit(solution)/shard_map/ppermute | solution.py:352
  151.3 2.5 %collective-permute-done.24 = f32[96,384]{1,0:T(8,128)S(1)} collective-permute-done((f32[96,384]{1,0:T(8,128)S(1)}, f32[96,384]{1,0:T(8,128)S(1)}, u32[]{:S(2)}, u32[]{:S(2)}) %collective-permute-start.24) | collective-permute-done | bytes 147488 | tf_op jit(solution)/shard_map/ppermute | solution.py:352
  (109 shorter events, 37.5 us)
Async XLA Ops:
  7.2 87.9 %all-gather.3.cloned.1.call-start = ((), (), s32[]{:S(2)}) async-start(), calls=%async_computation | async-start | bytes 2654208 | tf_op jit(solution)/shard_map/all_gather | solution.py:380
  8.7 22.1 %collective-permute-start.1 = (f32[480,384]{1,0:T(8,128)S(1)}, f32[480,384]{1,0:T(8,128)S(1)}, u32[]{:S(2)}, u32[]{:S(2)}) collective-permute-start(f32[480,384]{1,0:T(8,128)S(1)} %get-tuple-element.88), channel_id=1, source_target_pairs={{0,4},{1,5},{2,6},{3,7},{12,8},{13,9},{14,10},{15,11},{16,20},{17,... | collective-permute-start | bytes 2211848 | tf_op jit(solution)/shard_map/ppermute | solution.py:352
  11.7 38.9 %collective-permute-start.3 = (f32[480,384]{1,0:T(8,128)S(1)}, f32[480,384]{1,0:T(8,128)}, u32[]{:S(2)}, u32[]{:S(2)}) collective-permute-start(f32[480,384]{1,0:T(8,128)S(1)} %get-tuple-element.88), channel_id=1, source_target_pairs={{0,2},{1,3},{2,0},{3,1},{12,14},{13,15},{14,12},{15,13},{16,18},{1... | collective-permute-start | bytes 2211848 | tf_op jit(solution)/shard_map/ppermute | solution.py:352
  15.1 15.6 %collective-permute-start = (s32[3840]{0:T(1024)S(1)}, s32[3840]{0:T(1024)S(1)}, u32[]{:S(2)}, u32[]{:S(2)}) collective-permute-start(s32[3840]{0:T(1024)S(1)} %reduce), channel_id=1, source_target_pairs={{0,8},{8,0},{16,24},{24,16},{1,9},{9,1},{17,25},{25,17},{2,10},{10... | collective-permute-start | bytes 46088 | tf_op jit(solution)/shard_map/ppermute | solution.py:379
  15.2 35.4 %collective-permute-start.4 = (f32[480,384]{1,0:T(8,128)S(1)}, f32[480,384]{1,0:T(8,128)S(1)}, u32[]{:S(2)}, u32[]{:S(2)}) collective-permute-start(f32[480,384]{1,0:T(8,128)S(1)} %get-tuple-element.70), channel_id=1, source_target_pairs={{0,4},{1,5},{2,6},{3,7},{12,8},{13,9},{14,10},{15,11},{16,20},{17,... | collective-permute-start | bytes 2211848 | tf_op jit(solution)/shard_map/ppermute | solution.py:352
  30.8 22.3 %collective-permute-start.2 = (f32[480,384]{1,0:T(8,128)S(1)}, f32[480,384]{1,0:T(8,128)}, u32[]{:S(2)}, u32[]{:S(2)}) collective-permute-start(f32[480,384]{1,0:T(8,128)S(1)} %collective-permute-done.1.refs_0_), channel_id=1, source_target_pairs={{0,2},{1,3},{2,0},{3,1},{12,14},{13,15},{14,12},{15,13},{16,18},{1... | collective-permute-start | bytes 2211848 | tf_op jit(solution)/shard_map/ppermute | solution.py:352
  55.9 9.1 %collective-permute-start.7 = (f32[480,384]{1,0:T(8,128)S(1)}, f32[480,384]{1,0:T(8,128)S(1)}, u32[]{:S(2)}, u32[]{:S(2)}) collective-permute-start(f32[480,384]{1,0:T(8,128)S(1)} %collective-permute-done.1.refs_0_), channel_id=1, source_target_pairs={{0,1},{1,0},{2,3},{3,2},{12,13},{13,12},{14,15},{15,14},{16,17},{1... | collective-permute-start | bytes 2211848 | tf_op jit(solution)/shard_map/ppermute | solution.py:352
  58.0 8.0 %collective-permute-start.8 = (f32[480,384]{1,0:T(8,128)}, f32[480,384]{1,0:T(8,128)S(1)}, u32[]{:S(2)}, u32[]{:S(2)}) collective-permute-start(f32[480,384]{1,0:T(8,128)} %collective-permute-done.2.refs_2_), channel_id=1, source_target_pairs={{0,1},{1,0},{2,3},{3,2},{12,13},{13,12},{14,15},{15,14},{16,17},{1... | collective-permute-start | bytes 2211848 | tf_op jit(solution)/shard_map/ppermute | solution.py:352
  60.4 21.2 %collective-permute-start.9 = (f32[480,384]{1,0:T(8,128)S(1)}, f32[480,384]{1,0:T(8,128)S(1)}, u32[]{:S(2)}, u32[]{:S(2)}) collective-permute-start(f32[480,384]{1,0:T(8,128)S(1)} %collective-permute-done.4.refs_0_), channel_id=1, source_target_pairs={{0,2},{1,3},{2,0},{3,1},{12,14},{13,15},{14,12},{15,13},{16,18},{1... | collective-permute-start | bytes 2211848 | tf_op jit(solution)/shard_map/ppermute | solution.py:352
  62.8 20.7 %collective-permute-start.13 = (f32[480,384]{1,0:T(8,128)}, f32[480,384]{1,0:T(8,128)S(1)}, u32[]{:S(2)}, u32[]{:S(2)}) collective-permute-start(f32[480,384]{1,0:T(8,128)} %collective-permute-done.3), channel_id=1, source_target_pairs={{0,4},{1,5},{2,6},{3,7},{12,8},{13,9},{14,10},{15,11},{16,20},{17,... | collective-permute-start | bytes 2211848 | tf_op jit(solution)/shard_map/ppermute | solution.py:352
  64.2 23.9 %collective-permute-start.16 = (f32[480,384]{1,0:T(8,128)S(1)}, f32[480,384]{1,0:T(8,128)S(1)}, u32[]{:S(2)}, u32[]{:S(2)}) collective-permute-start(f32[480,384]{1,0:T(8,128)S(1)} %fusion.5), channel_id=1, source_target_pairs={{4,6},{5,7},{6,4},{7,5},{8,10},{9,11},{10,8},{11,9},{20,22},{21,23... | collective-permute-start | bytes 2211848 | tf_op jit(solution)/shard_map/ppermute | solution.py:352
  65.0 24.1 %collective-permute-start.12 = (f32[480,384]{1,0:T(8,128)S(1)}, f32[480,384]{1,0:T(8,128)S(1)}, u32[]{:S(2)}, u32[]{:S(2)}) collective-permute-start(f32[480,384]{1,0:T(8,128)S(1)} %fusion.6), channel_id=1, source_target_pairs={{4,6},{5,7},{6,4},{7,5},{8,10},{9,11},{10,8},{11,9},{20,22},{21,23... | collective-permute-start | bytes 2211848 | tf_op jit(solution)/shard_map/ppermute | solution.py:352
  66.0 51.5 %collective-permute-start.18 = (f32[480,384]{1,0:T(8,128)S(1)}, f32[480,384]{1,0:T(8,128)}, u32[]{:S(2)}, u32[]{:S(2)}) collective-permute-start(f32[480,384]{1,0:T(8,128)S(1)} %broadcast_select_fusion.1.refs_0_), channel_id=1, source_target_pairs={{0,2},{1,3},{2,0},{3,1},{4,6},{5,7},{6,4},{7,5},{8,10},{9,11},{10,... | collective-permute-start | bytes 2211848 | tf_op jit(solution)/shard_map/ppermute | solution.py:352
  81.7 8.5 %collective-permute-start.10 = (f32[480,384]{1,0:T(8,128)S(1)}, f32[480,384]{1,0:T(8,128)S(1)}, u32[]{:S(2)}, u32[]{:S(2)}) collective-permute-start(f32[480,384]{1,0:T(8,128)S(1)} %collective-permute-done.4.refs_0_), channel_id=1, source_target_pairs={{0,1},{1,0},{2,3},{3,2},{12,13},{13,12},{14,15},{15,14},{16,17},{1... | collective-permute-start | bytes 2211848 | tf_op jit(solution)/shard_map/ppermute | solution.py:352
  89.1 24.3 %collective-permute-start.17 = (f32[480,384]{1,0:T(8,128)}, f32[480,384]{1,0:T(8,128)}, u32[]{:S(2)}, u32[]{:S(2)}) collective-permute-start(f32[480,384]{1,0:T(8,128)} %fusion.2), channel_id=1, source_target_pairs={{4,0},{5,1},{6,2},{7,3},{8,12},{9,13},{10,14},{11,15},{20,16},{21,... | collective-permute-start | bytes 2211848 | tf_op jit(solution)/shard_map/ppermute | solution.py:352
  95.1 12.2 %collective-permute-start.14 = (f32[480,384]{1,0:T(8,128)S(1)}, f32[480,384]{1,0:T(8,128)}, u32[]{:S(2)}, u32[]{:S(2)}) collective-permute-start(f32[480,384]{1,0:T(8,128)S(1)} %broadcast_select_fusion.3.refs_0_), channel_id=1, source_target_pairs={{0,1},{1,0},{2,3},{3,2},{4,5},{5,4},{6,7},{7,6},{8,9},{9,8},{10,11... | collective-permute-start | bytes 2211848 | tf_op jit(solution)/shard_map/ppermute | solution.py:352
  95.1 12.2 %collective-permute-start.15 = (f32[480,384]{1,0:T(8,128)}, f32[480,384]{1,0:T(8,128)}, u32[]{:S(2)}, u32[]{:S(2)}) collective-permute-start(f32[480,384]{1,0:T(8,128)} %broadcast_select_fusion.2.refs_2_), channel_id=1, source_target_pairs={{0,1},{1,0},{2,3},{3,2},{4,5},{5,4},{6,7},{7,6},{8,9},{9,8},{10,11... | collective-permute-start | bytes 2211848 | tf_op jit(solution)/shard_map/ppermute | solution.py:352
  97.7 26.0 %collective-permute-start.19 = (f32[480,384]{1,0:T(8,128)}, f32[480,384]{1,0:T(8,128)}, u32[]{:S(2)}, u32[]{:S(2)}) collective-permute-start(f32[480,384]{1,0:T(8,128)} %broadcast_select_fusion), channel_id=1, source_target_pairs={{4,0},{5,1},{6,2},{7,3},{8,12},{9,13},{10,14},{11,15},{20,16},{21,... | collective-permute-start | bytes 2211848 | tf_op jit(solution)/shard_map/ppermute | solution.py:352
  124.2 13.9 %collective-permute-start.26 = (f32[4,96,384]{2,1,0:T(8,128)S(1)}, f32[4,96,384]{2,1,0:T(8,128)S(1)}, u32[]{:S(2)}, u32[]{:S(2)}) collective-permute-start(f32[4,96,384]{2,1,0:T(8,128)S(1)} %get-tuple-element.111), channel_id=1, source_target_pairs={{0,1},{1,0},{2,3},{3,2},{4,5},{5,4},{6,7},{7,6},{8,9},{9,8},{10,11... | collective-permute-start | bytes 1769480 | tf_op jit(solution)/shard_map/ppermute | solution.py:352
  138.7 9.6 %collective-permute-start.28 = (f32[96,384]{1,0:T(8,128)S(1)}, f32[96,384]{1,0:T(8,128)S(1)}, u32[]{:S(2)}, u32[]{:S(2)}) collective-permute-start(f32[96,384]{1,0:T(8,128)S(1)} %get-tuple-element.117), channel_id=1, source_target_pairs={{0,4},{1,5},{2,6},{3,7},{4,0},{5,1},{6,2},{7,3},{8,12},{9,13},{10,... | collective-permute-start | bytes 442376 | tf_op jit(solution)/shard_map/ppermute | solution.py:352
  139.3 9.0 %collective-permute-start.29 = (f32[96,384]{1,0:T(8,128)S(1)}, f32[96,384]{1,0:T(8,128)S(1)}, u32[]{:S(2)}, u32[]{:S(2)}) collective-permute-start(f32[96,384]{1,0:T(8,128)S(1)} %get-tuple-element.118), channel_id=1, source_target_pairs={{0,6},{1,7},{2,4},{3,5},{4,2},{5,3},{6,0},{7,1},{8,14},{9,15},{10,... | collective-permute-start | bytes 442376 | tf_op jit(solution)/shard_map/ppermute | solution.py:352
  141.8 9.5 %collective-permute-start.23 = (f32[96,384]{1,0:T(8,128)S(1)}, f32[96,384]{1,0:T(8,128)S(1)}, u32[]{:S(2)}, u32[]{:S(2)}) collective-permute-start(f32[96,384]{1,0:T(8,128)S(1)} %get-tuple-element.116), channel_id=1, source_target_pairs={{0,2},{1,3},{2,0},{3,1},{4,6},{5,7},{6,4},{7,5},{8,10},{9,11},{10,... | collective-permute-start | bytes 442376 | tf_op jit(solution)/shard_map/ppermute | solution.py:352
  142.4 11.4 %collective-permute-start.24 = (f32[96,384]{1,0:T(8,128)S(1)}, f32[96,384]{1,0:T(8,128)S(1)}, u32[]{:S(2)}, u32[]{:S(2)}) collective-permute-start(f32[96,384]{1,0:T(8,128)S(1)} %get-tuple-element.114), channel_id=1, source_target_pairs={{0,4},{1,5},{2,6},{3,7},{4,0},{5,1},{6,2},{7,3},{8,12},{9,13},{10,... | collective-permute-start | bytes 442376 | tf_op jit(solution)/shard_map/ppermute | solution.py:352
  144.9 8.9 %collective-permute-start.25 = (f32[96,384]{1,0:T(8,128)S(1)}, f32[96,384]{1,0:T(8,128)S(1)}, u32[]{:S(2)}, u32[]{:S(2)}) collective-permute-start(f32[96,384]{1,0:T(8,128)S(1)} %get-tuple-element.115), channel_id=1, source_target_pairs={{0,6},{1,7},{2,4},{3,5},{4,2},{5,3},{6,0},{7,1},{8,14},{9,15},{10,... | collective-permute-start | bytes 442376 | tf_op jit(solution)/shard_map/ppermute | solution.py:352
  (22 other events, 119.7 us)
Sparse Core Ops, SparseCore 0:
  33.4 32.1 all-gather.2
